TPU v7x, 256 devices: a whole 4x4x8 slice. The times are simulated.
256 devices in a mesh: tm: 16 (over z, core), space: 16 (over y, x).
Axes of the slice: x: 4, y: 4, z: 8, core: 2. Of those that a mesh axis runs over, the one named last changes fastest.
Arguments:
- volumes: float32 [16, 64, 512, 128], P('tm', 'space'), may hold values from -12 to 12
Outputs:
- corrected: float32 [16, 64, 512, 128], P('tm', 'space')
- shifts: float32 [16, 3], P('tm')
All inputs are finite; a program needn't handle non-finite values.
Results may differ from a plain program's by a relative error of at most 0.0003.
Values sent between devices are 32-bit elements; how exact they have to be, the bound alone decides.
A program may use at most 64 MiB of HBM per device.

v0:
```python
import math

import jax
import jax.numpy as jnp
from jax import lax
from jax.sharding import PartitionSpec as P

X = 512
Y = 128
Z = 64
ITERS = 2


precise = lax.Precision.HIGHEST
sharpness = 256.0
floor_share = 0.05


def dft_tables(length):
    indices = jnp.arange(length, dtype=jnp.int32)
    products = indices[:, None] * indices[None, :] % length
    angles = products.astype(jnp.float32) * (2.0 * math.pi / length)
    return (jnp.cos(angles), jnp.sin(angles))


def signed_freq(indices, length):
    wrapped = jnp.where(indices < length // 2, indices, indices - length)
    return jnp.where(indices == length // 2, 0, wrapped).astype(jnp.float32)


def centred(indices, length):
    return ((indices + length // 2) % length - length // 2).astype(jnp.float32)


def mix_z(table, data):
    return jnp.einsum("kz,vz...->vk...", table, data, precision=precise)


def mix_x(table, data):
    return jnp.einsum("kx,vzx...->vzk...", table, data, precision=precise)


def mix_y(data, table):
    return jnp.dot(data, table, precision=precise)


def forward(volume, tables):
    cos_x, sin_x, cos_y, sin_y, cos_z, sin_z = tables
    real_x = mix_x(cos_x, volume)
    imag_x = -mix_x(sin_x, volume)
    real_y = mix_y(real_x, cos_y) + mix_y(imag_x, sin_y)
    imag_y = mix_y(imag_x, cos_y) - mix_y(real_x, sin_y)
    real_p, imag_p = (
        lax.all_to_all(real_y, "space", split_axis=2, concat_axis=1, tiled=True),
        lax.all_to_all(imag_y, "space", split_axis=2, concat_axis=1, tiled=True),
    )
    real_z = mix_z(cos_z, real_p) + mix_z(sin_z, imag_p)
    imag_z = mix_z(cos_z, imag_p) - mix_z(sin_z, real_p)
    return (real_z, imag_z)


def inverse(spectrum, tables):
    cos_x, sin_x, cos_y, sin_y, cos_z, sin_z = tables
    norming = 1.0 / (X * Y * Z)
    real_in, imag_in = spectrum
    real_z = mix_z(cos_z, real_in) - mix_z(sin_z, imag_in)
    imag_z = mix_z(sin_z, real_in) + mix_z(cos_z, imag_in)
    real_y = mix_y(real_z, cos_y) - mix_y(imag_z, sin_y)
    imag_y = mix_y(real_z, sin_y) + mix_y(imag_z, cos_y)
    real_s, imag_s = (
        lax.all_to_all(real_y, "space", split_axis=1, concat_axis=2, tiled=True),
        lax.all_to_all(imag_y, "space", split_axis=1, concat_axis=2, tiled=True),
    )
    return (mix_x(cos_x, real_s) - mix_x(sin_x, imag_s)) * norming


def split_pairs(spectrum):
    return [(spectrum[0], spectrum[1])]


def join_pairs(pairs):
    return (pairs[0][0], pairs[0][1])


def y_frequencies():
    return [signed_freq(jnp.arange(Y, dtype=jnp.int32), Y)]


def template_sum(spectrum):
    return lax.psum((jnp.sum(spectrum[0], axis=0), jnp.sum(spectrum[1], axis=0)), "tm")


def weight_moments(weights, coords):
    coord_z, coord_x, coord_y = coords
    weight_sum = jnp.sum(weights, axis=(1, 2, 3))
    moment_z = jnp.sum(jnp.sum(weights, axis=(2, 3)) * coord_z[None, :], axis=1)
    moment_x = jnp.sum(jnp.sum(weights, axis=(1, 3)) * coord_x[None, :], axis=1)
    moment_y = jnp.sum(jnp.sum(weights, axis=(1, 2)) * coord_y[None, :], axis=1)
    return (weight_sum, jnp.stack([moment_z, moment_x, moment_y], axis=1))


def centroid(scores, coords):
    local_top = jnp.max(scores, axis=(1, 2, 3))
    top_score = lax.pmax(local_top, "space")
    weights = jnp.exp(scores - top_score[:, None, None, None])
    weight_sum, moments = weight_moments(weights, coords)
    weight_sum, moments = lax.psum((weight_sum, moments), "space")
    return moments / weight_sum[:, None]


def apply_ramp(real_in, imag_in, shifts, freq_z, freq_x, freq_y):
    phases = (
        2.0
        * math.pi
        * (
            freq_z[None, :, None] * (shifts[:, 0] / Z)[:, None, None]
            + freq_x[None, None, :] * (shifts[:, 1] / X)[:, None, None]
        )
    )
    phases = (
        phases[..., None]
        + 2.0 * math.pi * freq_y[None, None, None, :] * (shifts[:, 2] / Y)[:, None, None, None]
    )
    cosine = jnp.cos(phases)
    sine = jnp.sin(phases)
    return (real_in * cosine - imag_in * sine, real_in * sine + imag_in * cosine)


def whiten(spec_re, spec_im, tmpl_re, tmpl_im):
    prod_re = spec_re * tmpl_re + spec_im * tmpl_im
    prod_im = spec_im * tmpl_re - spec_re * tmpl_im
    divisor = jnp.maximum(
        jnp.sqrt(prod_re * prod_re + prod_im * prod_im), floor_share * (X * Y * Z)
    )
    return (prod_re / divisor, prod_im / divisor)


def body(volumes):
    position = lax.axis_index("space")
    slab_depth = volumes.shape[1]
    pencil = X // lax.axis_size("space")
    frames = volumes.shape[0] * lax.axis_size("tm")
    tables = dft_tables(X) + dft_tables(Y) + dft_tables(Z)
    z_index = position * slab_depth + jnp.arange(slab_depth, dtype=jnp.int32)
    x_index = position * pencil + jnp.arange(pencil, dtype=jnp.int32)
    coords = (
        centred(z_index, Z),
        centred(jnp.arange(X, dtype=jnp.int32), X),
        centred(jnp.arange(Y, dtype=jnp.int32), Y),
    )
    freq_z = signed_freq(jnp.arange(Z, dtype=jnp.int32), Z)
    freq_x = signed_freq(x_index, X)
    freq_ys = y_frequencies()
    spectrum = forward(volumes, tables)
    spec_pairs = split_pairs(spectrum)
    shifted = spectrum
    for iteration in range(ITERS):
        summed = template_sum(shifted)
        template = tuple((part[None] / frames for part in summed))
        tmpl_pairs = split_pairs(template)
        white_pairs = [
            whiten(spec_pairs[0][0], spec_pairs[0][1], tmpl_pairs[0][0], tmpl_pairs[0][1])
        ]
        correlation = inverse(join_pairs(white_pairs), tables)
        shifts = centroid(sharpness * correlation, coords)
        ramped = [
            apply_ramp(spec_pairs[0][0], spec_pairs[0][1], shifts, freq_z, freq_x, freq_ys[0])
        ]
        shifted = join_pairs(ramped)
    corrected = inverse(shifted, tables)
    return (corrected, shifts)


def solution(mesh):
    in_specs = (P("tm", "space", None, None),)
    out_specs = (P("tm", "space", None, None), P("tm", None))
    return jax.shard_map(body, mesh=mesh, in_specs=in_specs, out_specs=out_specs, check_vma=False)
```

profile of v0, /device:TPU:96, one launch (start us, length us, event | category | flops | bytes accessed | tf_op | source)
XLA Modules:
  0.0 713.9 jit_solution(18207688949211915595)
XLA Ops:
  8.4 5.7 fusion.26
  14.1 5.7 convolution_bitcast_fusion
  24.4 7.1 all-to-all-start
  35.5 13.6 %all-to-all-done = f32[1,4,512,128]{3,1,0,2:T(4,128)} async-done(((f32[1,4,512,128]{3,1,0,2:T(4,128)}), f32[1,4,512,128]{3,1,0,2:T(4,128)}, u32[]{:S(2)}, u32[]{:S(2)}) %all-to-all-start) | async-done | bytes 1048608 | tf_op jit(solution)/shard_map/all_to_all | solution.py:54
  49.2 3.7 all-to-all-start.1
  54.4 14.8 %all-to-all-done.1 = f32[1,4,512,128]{3,1,0,2:T(4,128)S(1)} async-done(((f32[1,4,512,128]{3,1,0,2:T(4,128)}), f32[1,4,512,128]{3,1,0,2:T(4,128)S(1)}, u32[]{:S(2)}, u32[]{:S(2)}) %all-to-all-start.1) | async-done | bytes 1048608 | tf_op jit(solution)/shard_map/all_to_all | solution.py:55
  76.1 112.1 %all-reduce.9.cloned.1.call-done = (f32[64,32,128]{2,0,1:T(8,128)}, f32[64,32,128]{2,0,1:T(8,128)}) async-done(((f32[64,32,128]{2,0,1:T(8,128)}, f32[64,32,128]{2,0,1:T(8,128)}), (f32[64,32,128]{2,0,1:T(8,128)}, f32[64,32,128]{2,0,1:T(8,128)})) %all-reduce.9.cloned.1.call-update) | async-done | bytes 2097168 | tf_op jit(solution)/shard_map/psum | solution.py:90
  201.7 6.9 all-to-all-start.3
  214.3 15.1 %all-to-all-done.3 = f32[1,64,32,128]{3,2,0,1:T(8,128)} async-done(((f32[1,64,32,128]{3,2,0,1:T(8,128)}), f32[1,64,32,128]{3,2,0,1:T(8,128)}, u32[]{:S(2)}, u32[]{:S(2)}) %all-to-all-start.3) | async-done | bytes 1048608 | tf_op jit(solution)/shard_map/all_to_all | solution.py:72
  235.7 15.2 %all-to-all-done.2 = f32[1,64,32,128]{3,2,0,1:T(8,128)S(1)} async-done(((f32[1,64,32,128]{3,2,0,1:T(8,128)}), f32[1,64,32,128]{3,2,0,1:T(8,128)S(1)}, u32[]{:S(2)}, u32[]{:S(2)}) %all-to-all-start.2) | async-done | bytes 1048608 | tf_op jit(solution)/shard_map/all_to_all | solution.py:71
  251.0 7.5 %fusion.64 = f32[4,128,512]{2,1,0:T(8,128)S(1)} fusion(f32[4,512,128]{2,1,0:T(8,128)S(1)} %bitcast.345), kind=kOutput, calls=%fused_computation.100 | convolution fusion | flops 1614282752 | bytes 2097152 | tf_op jit(solution)/shard_map/kx,vzx...->vzk.../dot_general | solution.py:40
  258.5 8.2 %fusion.382 = (f32[]{:T(128)}, f32[4,128,512]{2,1,0:T(8,128)S(1)}) fusion(f32[4,128,512]{2,1,0:T(8,128)S(1)} %fusion.64, f32[4,512,128]{2,1,0:T(8,128)S(1)} %bitcast.342), kind=kOutput, calls=%fused_computation.411 | convolution fusion | flops 1615069184 | bytes 3145732 | tf_op jit(solution)/shard_map/kx,vzx...->vzk.../dot_general | solution.py:40
  266.7 37.4 %pmax.14 = f32[]{:T(128)} all-reduce(f32[]{:T(128)} %get-tuple-element.38), channel_id=1, replica_groups=mesh['tm'=16,'space'=16] {'space'}, use_global_device_ids=true, to_apply=%region_3.4 | all-reduce | flops 1 | bytes 8 | tf_op jit(solution)/shard_map/pmax | solution.py:104
  309.6 37.2 %all-reduce.1 = (f32[1,3]{1,0:T(1,128)S(1)}, f32[]{:T(128)}) all-reduce(f32[1,3]{1,0:T(1,128)S(1)} %pad_maximum_fusion, f32[]{:T(128)} %get-tuple-element.14), channel_id=1, replica_groups=mesh['tm'=16,'space'=16] {'space'}, use_global_device_ids=true, to_apply=%region_10.11 | all-reduce | flops 4 | bytes 32 | tf_op jit(solution)/shard_map/psum | solution.py:107
  350.2 5.6 fusion.32
  355.8 109.1 %all-reduce.7.cloned.1.call-done = (f32[64,32,128]{2,0,1:T(8,128)}, f32[64,32,128]{2,0,1:T(8,128)}) async-done(((f32[64,32,128]{2,0,1:T(8,128)}, f32[64,32,128]{2,0,1:T(8,128)}), (f32[64,32,128]{2,0,1:T(8,128)}, f32[64,32,128]{2,0,1:T(8,128)})) %all-reduce.7.cloned.1.call-update) | async-done | bytes 2097168 | tf_op jit(solution)/shard_map/psum | solution.py:90
  478.2 7.0 all-to-all-start.5
  491.0 15.2 %all-to-all-done.5 = f32[1,64,32,128]{3,2,0,1:T(8,128)} async-done(((f32[1,64,32,128]{3,2,0,1:T(8,128)}), f32[1,64,32,128]{3,2,0,1:T(8,128)}, u32[]{:S(2)}, u32[]{:S(2)}) %all-to-all-start.5) | async-done | bytes 1048608 | tf_op jit(solution)/shard_map/all_to_all | solution.py:72
  512.2 15.4 %all-to-all-done.4 = f32[1,64,32,128]{3,2,0,1:T(8,128)S(1)} async-done(((f32[1,64,32,128]{3,2,0,1:T(8,128)}), f32[1,64,32,128]{3,2,0,1:T(8,128)S(1)}, u32[]{:S(2)}, u32[]{:S(2)}) %all-to-all-start.4) | async-done | bytes 1048608 | tf_op jit(solution)/shard_map/all_to_all | solution.py:71
  527.8 7.5 %fusion.62 = f32[4,128,512]{2,1,0:T(8,128)S(1)} fusion(f32[4,512,128]{2,1,0:T(8,128)S(1)} %bitcast.346), kind=kOutput, calls=%fused_computation.98 | convolution fusion | flops 1614282752 | bytes 2097152 | tf_op jit(solution)/shard_map/kx,vzx...->vzk.../dot_general | solution.py:40
  535.3 8.2 %fusion.383 = (f32[]{:T(128)}, f32[4,128,512]{2,1,0:T(8,128)S(1)}) fusion(f32[4,128,512]{2,1,0:T(8,128)S(1)} %fusion.62, f32[4,512,128]{2,1,0:T(8,128)S(1)} %bitcast.343), kind=kOutput, calls=%fused_computation.412 | convolution fusion | flops 1615069184 | bytes 3145732 | tf_op jit(solution)/shard_map/kx,vzx...->vzk.../dot_general | solution.py:40
  543.5 37.4 %pmax.15 = f32[]{:T(128)} all-reduce(f32[]{:T(128)} %get-tuple-element.40), channel_id=1, replica_groups=mesh['tm'=16,'space'=16] {'space'}, use_global_device_ids=true, to_apply=%region_16.17 | all-reduce | flops 1 | bytes 8 | tf_op jit(solution)/shard_map/pmax | solution.py:104
  586.4 36.8 %all-reduce = (f32[1,3]{1,0:T(1,128)S(1)}, f32[]{:T(128)}) all-reduce(f32[1,3]{1,0:T(1,128)S(1)} %pad_maximum_fusion.1, f32[]{:T(128)} %get-tuple-element.10), channel_id=1, replica_groups=mesh['tm'=16,'space'=16] {'space'}, use_global_device_ids=true, to_apply=%region_23.24 | all-reduce | flops 4 | bytes 32 | tf_op jit(solution)/shard_map/psum | solution.py:107
  626.6 5.0 fusion.112
  631.6 5.0 fusion.114
  636.6 5.2 fusion.12
  641.8 5.0 fusion.13
  651.6 3.8 all-to-all-start.7
  660.0 13.2 %all-to-all-done.7 = f32[1,64,32,128]{3,2,0,1:T(8,128)S(1)} async-done(((f32[1,64,32,128]{3,2,0,1:T(8,128)}), f32[1,64,32,128]{3,2,0,1:T(8,128)S(1)}, u32[]{:S(2)}, u32[]{:S(2)}) %all-to-all-start.7) | async-done | bytes 1048608 | tf_op jit(solution)/shard_map/all_to_all | solution.py:72
  676.9 13.2 %all-to-all-done.6 = f32[1,64,32,128]{3,2,0,1:T(8,128)S(1)} async-done(((f32[1,64,32,128]{3,2,0,1:T(8,128)}), f32[1,64,32,128]{3,2,0,1:T(8,128)S(1)}, u32[]{:S(2)}, u32[]{:S(2)}) %all-to-all-start.6) | async-done | bytes 1048608 | tf_op jit(solution)/shard_map/all_to_all | solution.py:71
  690.2 7.5 %fusion.60 = f32[4,128,512]{2,1,0:T(8,128)S(1)} fusion(f32[4,512,128]{2,1,0:T(8,128)S(1)} %bitcast.347), kind=kOutput, calls=%fused_computation.96 | convolution fusion | flops 1614282752 | bytes 2097152 | tf_op jit(solution)/shard_map/kx,vzx...->vzk.../dot_general | solution.py:40
  697.8 7.6 %fusion.9 = f32[1,4,512,128]{2,3,1,0:T(8,128)S(1)} fusion(f32[4,128,512]{2,1,0:T(8,128)S(1)} %fusion.60, f32[4,512,128]{2,1,0:T(8,128)S(1)} %bitcast.344), kind=kOutput, calls=%fused_computation.17 | convolution fusion | flops 1614807040 | bytes 3145728 | tf_op jit(solution)/shard_map/kx,vzx...->vzk.../dot_general | solution.py:40
  (92 shorter events, 97.2 us)
Async XLA Ops:
  7.2 1.2 copy-start
  24.4 24.8 %all-to-all-start = ((f32[1,4,512,128]{3,1,0,2:T(4,128)}), f32[1,4,512,128]{3,1,0,2:T(4,128)}, u32[]{:S(2)}, u32[]{:S(2)}) async-start(f32[1,4,512,128]{3,1,0,2:T(4,128)} %copy.80), calls=%async_computation | async-start | bytes 2097152 | tf_op jit(solution)/shard_map/all_to_all | solution.py:54
  49.2 20.0 %all-to-all-start.1 = ((f32[1,4,512,128]{3,1,0,2:T(4,128)}), f32[1,4,512,128]{3,1,0,2:T(4,128)S(1)}, u32[]{:S(2)}, u32[]{:S(2)}) async-start(f32[1,4,512,128]{3,1,0,2:T(4,128)} %copy.82), calls=%async_computation.1 | async-start | bytes 2097152 | tf_op jit(solution)/shard_map/all_to_all | solution.py:55
  52.8 135.4 %all-reduce.9.cloned.1.call-start = ((), (), s32[]{:S(2)}) async-start(), calls=%async_computation.9 | async-start | bytes 4194304 | tf_op jit(solution)/shard_map/psum | solution.py:90
  76.1 112.1 %copy-start.2 = (f32[32,128,64]{1,2,0:T(8,128)S(1)}, f32[32,128,64]{1,2,0:T(8,128)}, u32[]{:S(2)}) copy-start(f32[32,128,64]{1,2,0:T(8,128)} %convolution_subtract_fusion.9) | copy-start | bytes 3145732
  76.1 112.1 %copy-start.3 = (f32[32,128,64]{1,2,0:T(8,128)S(1)}, f32[32,128,64]{1,2,0:T(8,128)}, u32[]{:S(2)}) copy-start(f32[32,128,64]{1,2,0:T(8,128)} %convolution_add_fusion.6) | copy-start | bytes 3145732
  197.1 1.8 copy-start.6
  201.7 27.7 %all-to-all-start.3 = ((f32[1,64,32,128]{3,2,0,1:T(8,128)}), f32[1,64,32,128]{3,2,0,1:T(8,128)}, u32[]{:S(2)}, u32[]{:S(2)}) async-start(f32[1,64,32,128]{3,2,0,1:T(8,128)} %fusion.20), calls=%async_computation.3 | async-start | bytes 2097152 | tf_op jit(solution)/shard_map/all_to_all | solution.py:72
  229.4 21.4 %all-to-all-start.2 = ((f32[1,64,32,128]{3,2,0,1:T(8,128)}), f32[1,64,32,128]{3,2,0,1:T(8,128)S(1)}, u32[]{:S(2)}, u32[]{:S(2)}) async-start(f32[1,64,32,128]{3,2,0,1:T(8,128)} %fusion.21), calls=%async_computation.2 | async-start | bytes 2097152 | tf_op jit(solution)/shard_map/all_to_all | solution.py:71
  233.1 231.8 %all-reduce.7.cloned.1.call-start = ((), (), s32[]{:S(2)}) async-start(), calls=%async_computation.8 | async-start | bytes 4194304 | tf_op jit(solution)/shard_map/psum | solution.py:90
  251.0 7.5 %copy-start.8 = (f32[1,4,16,32,128]{4,3,2,1,0:T(8,128)S(1)}, f32[1,4,16,32,128]{4,3,2,1,0:T(8,128)}, u32[]{:S(2)}) copy-start(f32[1,4,16,32,128]{4,3,2,1,0:T(8,128)} %copy.92) | copy-start | bytes 3145732
  473.6 1.8 copy-start.7
  478.2 28.0 %all-to-all-start.5 = ((f32[1,64,32,128]{3,2,0,1:T(8,128)}), f32[1,64,32,128]{3,2,0,1:T(8,128)}, u32[]{:S(2)}, u32[]{:S(2)}) async-start(f32[1,64,32,128]{3,2,0,1:T(8,128)} %fusion.15), calls=%async_computation.5 | async-start | bytes 2097152 | tf_op jit(solution)/shard_map/all_to_all | solution.py:72
  506.2 21.5 %all-to-all-start.4 = ((f32[1,64,32,128]{3,2,0,1:T(8,128)}), f32[1,64,32,128]{3,2,0,1:T(8,128)S(1)}, u32[]{:S(2)}, u32[]{:S(2)}) async-start(f32[1,64,32,128]{3,2,0,1:T(8,128)} %fusion.16), calls=%async_computation.4 | async-start | bytes 2097152 | tf_op jit(solution)/shard_map/all_to_all | solution.py:71
  527.8 7.5 %copy-start.9 = (f32[1,4,16,32,128]{4,3,2,1,0:T(8,128)S(1)}, f32[1,4,16,32,128]{4,3,2,1,0:T(8,128)}, u32[]{:S(2)}) copy-start(f32[1,4,16,32,128]{4,3,2,1,0:T(8,128)} %copy.102) | copy-start | bytes 3145732
  623.8 0.7 copy-start.10
  646.8 1.8 copy-start.4
  651.6 3.8 copy-start.5
  651.6 21.5 %all-to-all-start.7 = ((f32[1,64,32,128]{3,2,0,1:T(8,128)}), f32[1,64,32,128]{3,2,0,1:T(8,128)S(1)}, u32[]{:S(2)}, u32[]{:S(2)}) async-start(f32[1,64,32,128]{3,2,0,1:T(8,128)} %fusion.10), calls=%async_computation.7 | async-start | bytes 2097152 | tf_op jit(solution)/shard_map/all_to_all | solution.py:72
  673.2 17.0 %all-to-all-start.6 = ((f32[1,64,32,128]{3,2,0,1:T(8,128)}), f32[1,64,32,128]{3,2,0,1:T(8,128)S(1)}, u32[]{:S(2)}, u32[]{:S(2)}) async-start(f32[1,64,32,128]{3,2,0,1:T(8,128)} %fusion.11), calls=%async_computation.6 | async-start | bytes 2097152 | tf_op jit(solution)/shard_map/all_to_all | solution.py:71
  697.7 8.9 %copy-start.1 = (f32[1,4,512,128]{3,2,1,0:T(8,128)S(1)}, f32[1,4,512,128]{3,2,1,0:T(8,128)}, u32[]{:S(2)}) copy-start(f32[1,4,512,128]{3,2,1,0:T(8,128)} %param.1) | copy-start | bytes 3145732
Sparse Core Ops, SparseCore 0:
  76.2 111.9 all-reduce.8
  355.9 108.8 all-reduce.6
where the time goes:
time: 724 us; the launch traced here: 714 us
  waiting for transfers between devices  337 us (47%)
  blocking collectives  149 us (21%)
  matrix products  133 us (18%)
  starting transfers between devices  39.7 us (5%)
  other arithmetic  22.1 us (3%)
  between operations  18.9 us (3%)
  local copies, waits for them, and re-layouts  14.1 us (2%)
    psum x2, waiting for transfers between devices, template_sum(): lax.psum((jnp.sum(spectrum[0], axis=0), jnp.sum(spectrum[1], axis=0)), 'tm')  221 us
    pmax x2, blocking collectives, centroid(): top_score = lax.pmax(local_top, 'space')  74.8 us
    psum x2, blocking collectives, centroid(): weight_sum, moments = lax.psum((weight_sum, moments), 'space')  74 us
    dot_general x8, matrix products, mix_x(): return jnp.einsum('kx,vzx...->vzk...', table, data, precision=precise)  57.9 us
    all_to_all x3, waiting for transfers between devices, inverse(): lax.all_to_all(real_y, 'space', split_axis=1, concat_axis=2, tiled=True)  43.8 us
    all_to_all x3, waiting for transfers between devices, inverse(): lax.all_to_all(imag_y, 'space', split_axis=1, concat_axis=2, tiled=True)  43.5 us
    dot_general x16, matrix products, mix_z(): return jnp.einsum('kz,vz...->vk...', table, data, precision=precise)  40.3 us
    dot_general x16, matrix products, mix_y(): return jnp.dot(data, table, precision=precise)  35.3 us
  transfers between devices with their start and end apart: 10, of which 10 were waited for; matrix products, arithmetic and copies ran while one was open for 4% of the time, Pallas kernels for 0%

commit v1 on v0

v1 whole, which is shorter than its diff:
```python
import functools
import math

import jax
import jax.numpy as jnp
import ml_dtypes
import numpy as np
from jax import lax
from jax.experimental import pallas as pl
from jax.experimental.pallas import tpu as pltpu
from jax.sharding import PartitionSpec as P

X = 512
Y = 128
Z = 64
ITERS = 2
FRAMES = 16
SHARPNESS = 256.0
FLOOR = 0.05 * (X * Y * Z)

SPACE = 16
CHIPS = 8
SLABS = Z // SPACE
SLOTS = X // 2 // SPACE
ROWS = SPACE * SLOTS * 8
MSG = SLOTS * 8
UNIT = 2 * Z + 8
NQ = 4
PART = MSG // NQ
PAIRS = SLOTS // 2 // NQ
MESH = pl.DeviceIdType.MESH
F32 = jnp.float32
BF16 = jnp.bfloat16


def tables():
    def angles(n, rows, columns):
        return 2.0 * np.pi * ((rows[:, None] * columns[None, :]) % n) / n

    half = X // 2
    a = angles(X, np.arange(half), np.arange(X))
    sign = (-1.0) ** np.arange(X)
    cos_x, sin_x = np.cos(a), np.sin(a)
    im = -sin_x
    im[0] = sign
    forward_x = np.concatenate([cos_x, im])
    weight = np.full((X, 1), 2.0)
    weight[0] = weight[half] = 1.0
    inverse_x = (forward_x * weight).T / (X * Y * Z)

    a = angles(Y, np.arange(Y), np.arange(Y))
    c, s = np.cos(a), np.sin(a)
    forward_y = np.block([[c, -s], [s, c]])
    inverse_y = np.block([[c, s], [-s, c]])

    a = angles(Z, np.arange(Z), np.arange(Z))
    c, s = np.cos(a), np.sin(a)
    forward_z = np.block([[c, s], [-s, c]])
    inverse_z = np.block([[c, -s], [s, c]])
    order = np.arange(2 * Z).reshape(2, SPACE, SLABS).transpose(1, 0, 2).reshape(-1)
    forward_z = forward_z[:, order]
    inverse_z = inverse_z[order, :]

    out = []
    for table in (forward_x, inverse_x, forward_y, inverse_y, forward_z, inverse_z):
        high = table.astype(np.float32).astype(ml_dtypes.bfloat16)
        low = (table - high.astype(np.float64)).astype(np.float32).astype(ml_dtypes.bfloat16)
        out += [high, low]
    return out


def split(value):
    high = value.astype(BF16)
    return high, (value - high.astype(F32)).astype(BF16)


def dot(a, b):
    return jnp.dot(a, b, preferred_element_type=F32)


def table_dot(high, low, data):
    data_high, data_low = split(data)
    return dot(high, data_high) + (dot(high, data_low) + dot(low, data_high))


def dot_table(data, high, low):
    data_high, data_low = split(data)
    return dot(data_high, high) + (dot(data_low, high) + dot(data_high, low))


def rows_of(start, count):
    return pl.ds(pl.multiple_of(start, 8), count)


def signed(index, n):
    wrapped = jnp.where(index < n // 2, index, index - n)
    return jnp.where(index == n // 2, 0, wrapped).astype(F32)


def kernel(
    v_ref, fxh, fxl, ixh, ixl, fyh, fyl, iyh, iyl, fzh, fzl, izh, izl,
    out_ref, shift_ref,
    send_f, recv_f, spec, moved, other, pair, ring_r, ring_l, sent_r, sent_l, tmpl,
    send_i, recv_i, scores, stats_out, stats_in, ramp_zy, ramp_x,
    fwd_send, fwd_recv, inv_send, inv_recv, st_send, st_recv,
    oc_send, oc_recv, rr_send, rr_recv, rl_send, rl_recv,
    gr_send, gr_recv, gl_send, gl_recv, go_send, go_recv,
):
    s = lax.axis_index("space")
    t = lax.axis_index("tm")
    core = t % 2
    chip = t // 2
    mate = chip * 2 + 1 - core
    right = ((chip + 1) % CHIPS) * 2 + core
    left = ((chip + CHIPS - 1) % CHIPS) * 2 + core

    barrier = pltpu.get_barrier_semaphore()

    def greet(i, carry):
        pl.semaphore_signal(barrier, inc=1, device_id={"space": (s + i) % SPACE}, device_id_type=MESH)
        return carry

    lax.fori_loop(1, SPACE, greet, 0)
    for member in (mate, right, left):
        pl.semaphore_signal(barrier, inc=1, device_id={"tm": member}, device_id_type=MESH)

    row = lax.broadcasted_iota(jnp.int32, (2 * Z, 128), 0)
    first_part = (row // SLABS) % 2 == 0

    def to_space(source, start, target, target_start, send_sem, recv_sem, device, count):
        return pltpu.make_async_remote_copy(
            src_ref=source.at[rows_of(start, count)],
            dst_ref=target.at[rows_of(target_start, count)],
            send_sem=send_sem,
            recv_sem=recv_sem,
            device_id={"space": device},
            device_id_type=MESH,
        )

    for z in range(0, SLABS, 2):
        data = jnp.concatenate([v_ref[z], v_ref[z + 1]], axis=1)
        result = table_dot(fxh[...], fxl[...], data)
        for i in range(2):
            for part in range(2):
                send_f[pl.ds(part * SLABS + z + i, X // 2, stride=8), :] = result[
                    part * (X // 2) : (part + 1) * (X // 2), i * 128 : (i + 1) * 128
                ]

    pl.semaphore_wait(barrier, SPACE + 2)

    def exchange_part(source, target, send_sem, recv_sem, q):
        def one(i, carry):
            d = (s + i) % SPACE
            to_space(
                source, d * MSG + q * PART, target, s * MSG + q * PART,
                send_sem.at[q, d], recv_sem.at[q, s], d, PART,
            ).start()
            return carry

        lax.fori_loop(1, SPACE, one, 0)
        mine = rows_of(s * MSG + q * PART, PART)
        target[mine, :] = source[mine, :]

    def wait_part(source, target, send_sem, recv_sem, q):
        def one(i, carry):
            d = (s + i) % SPACE
            to_space(
                source, d * MSG + q * PART, target, d * MSG + q * PART,
                send_sem.at[q, d], recv_sem.at[q, d], d, PART,
            ).wait_recv()
            return carry

        lax.fori_loop(1, SPACE, one, 0)

    def wait_sent(source, target, send_sem, recv_sem, q):
        def one(i, carry):
            d = (s + i) % SPACE
            to_space(
                source, d * MSG + q * PART, target, s * MSG + q * PART,
                send_sem.at[q, d], recv_sem.at[q, s], d, PART,
            ).wait_send()
            return carry

        lax.fori_loop(1, SPACE, one, 0)

    def send_all(q, carry):
        exchange_part(send_f, recv_f, fwd_send, fwd_recv, q)
        return carry

    lax.fori_loop(0, NQ, send_all, 0)

    def load_slot(j):
        return jnp.concatenate([recv_f[rows_of(d * MSG + j * 8, 8), :] for d in range(SPACE)], axis=0)

    def complex_rows(value):
        return jnp.concatenate([value[:Z], value[Z:]], axis=1)

    def part_rows(value):
        return jnp.concatenate([value[:, :128], value[:, 128:]], axis=0)

    def spectrum_pair(i, carry):
        j = 2 * i
        keep = jnp.where(first_part, 1.0, jnp.where(s + j == 0, 0.0, 1.0))
        data = jnp.concatenate([load_slot(j) * keep, load_slot(j + 1)], axis=1)
        zed = table_dot(fzh[...], fzl[...], data)
        lines = jnp.concatenate([complex_rows(zed[:, :128]), complex_rows(zed[:, 128:])], axis=0)
        freq = dot_table(lines, fyh[...], fyl[...])
        spec[j, 0 : 2 * Z, :] = part_rows(freq[:Z])
        spec[j + 1, 0 : 2 * Z, :] = part_rows(freq[Z:])
        return carry

    def forward_part(q, carry):
        wait_part(send_f, recv_f, fwd_send, fwd_recv, q)
        return lax.fori_loop(q * PAIRS, (q + 1) * PAIRS, spectrum_pair, carry)

    lax.fori_loop(0, NQ, forward_part, 0)

    slot = load_slot(0)
    slot = jnp.concatenate([slot[SLABS:], slot[:SLABS]], axis=0)
    slot = slot * jnp.where(first_part, jnp.where(s == 0, 1.0, 0.0), 0.0)
    freq = dot_table(complex_rows(table_dot(fzh[...], fzl[...], slot)), fyh[...], fyl[...])
    freq = part_rows(freq)
    for u in range(SLOTS):
        spec[u, 2 * Z :, :] = freq[8 * u : 8 * u + 8]

    base = core * CHIPS
    sends = []

    def to_tm(source, target, send_sem, recv_sem, device):
        return pltpu.make_async_remote_copy(
            src_ref=source,
            dst_ref=target,
            send_sem=send_sem,
            recv_sem=recv_sem,
            device_id={"tm": device},
            device_id_type=MESH,
        )

    def start(copy):
        copy.start()
        sends.append(copy)

    def template_sum(it, source):
        copy = to_tm(
            source.at[pl.ds((1 - core) * CHIPS, CHIPS)], other.at[it], oc_send.at[it], oc_recv.at[it], mate
        )
        start(copy)
        copy.wait_recv()

        def add(u, carry):
            pair[it, u] = source[base + u] + other[it, u]
            return carry

        lax.fori_loop(0, CHIPS, add, 0)
        for k in range(4):
            unit = (chip + 4 - k) % CHIPS
            if k == 0:
                outgoing = pair.at[it, unit]
            else:
                to_tm(sent_r.at[it, k], ring_r.at[it, k - 1], rr_send.at[it, k - 1], rr_recv.at[it, k - 1], left).wait_recv()
                sent_r[it, k] = pair[it, unit] + ring_r[it, k - 1]
                outgoing = sent_r.at[it, k]
            start(to_tm(outgoing, ring_r.at[it, k], rr_send.at[it, k], rr_recv.at[it, k], right))
            if k < 3:
                unit = (chip + CHIPS - 3 + k) % CHIPS
                if k == 0:
                    outgoing = pair.at[it, unit]
                else:
                    to_tm(sent_l.at[it, k], ring_l.at[it, k - 1], rl_send.at[it, k - 1], rl_recv.at[it, k - 1], right).wait_recv()
                    sent_l[it, k] = pair[it, unit] + ring_l[it, k - 1]
                    outgoing = sent_l.at[it, k]
                start(to_tm(outgoing, ring_l.at[it, k], rl_send.at[it, k], rl_recv.at[it, k], left))
        to_tm(ring_r.at[it, 3], ring_r.at[it, 3], rr_send.at[it, 3], rr_recv.at[it, 3], left).wait_recv()
        to_tm(ring_l.at[it, 2], ring_l.at[it, 2], rl_send.at[it, 2], rl_recv.at[it, 2], right).wait_recv()
        tmpl[it, base + chip] = (pair[it, chip] + (ring_r[it, 3] + ring_l[it, 2])) * (1.0 / FRAMES)

        def to_mate(unit):
            ref = tmpl.at[it, base + unit]
            start(to_tm(ref, ref, go_send.at[it, unit], go_recv.at[it, unit], mate))

        for k in range(4):
            unit = (chip + CHIPS - k) % CHIPS
            ref = tmpl.at[it, base + unit]
            if k > 0:
                to_tm(ref, ref, gr_send.at[it, k - 1], gr_recv.at[it, k - 1], left).wait_recv()
            start(to_tm(ref, ref, gr_send.at[it, k], gr_recv.at[it, k], right))
            if k < 3:
                unit_l = (chip + k) % CHIPS
                ref_l = tmpl.at[it, base + unit_l]
                if k > 0:
                    to_tm(ref_l, ref_l, gl_send.at[it, k - 1], gl_recv.at[it, k - 1], right).wait_recv()
                start(to_tm(ref_l, ref_l, gl_send.at[it, k], gl_recv.at[it, k], left))
                if k > 0:
                    to_mate(unit_l)
            to_mate(unit)
        unit = (chip + 4) % CHIPS
        ref = tmpl.at[it, base + unit]
        to_tm(ref, ref, gr_send.at[it, 3], gr_recv.at[it, 3], left).wait_recv()
        to_mate(unit)
        unit = (chip + 3) % CHIPS
        ref = tmpl.at[it, base + unit]
        to_tm(ref, ref, gl_send.at[it, 2], gl_recv.at[it, 2], right).wait_recv()
        to_mate(unit)
        for u in range(CHIPS):
            ref = tmpl.at[it, (1 - core) * CHIPS + u]
            to_tm(ref, ref, go_send.at[it, u], go_recv.at[it, u], mate).wait_recv()

    def whiten(f_re, f_im, t_re, t_im):
        p_re = f_re * t_re + f_im * t_im
        p_im = f_im * t_re - f_re * t_im
        scale = lax.rsqrt(jnp.maximum(p_re * p_re + p_im * p_im, FLOOR * FLOOR))
        return p_re * scale, p_im * scale

    def slot_of(ref, j):
        return ref[j, 0:Z, :], ref[j, Z : 2 * Z, :]

    def last_slot(ref):
        value = jnp.concatenate([ref[u, 2 * Z :, :] for u in range(SLOTS)], axis=0)
        return value[:Z], value[Z:]

    def inverse(n, slot_values, last_values):
        def back(values):
            lines = [jnp.concatenate([re, im], axis=1) for re, im in values]
            lines = dot_table(jnp.concatenate(lines, axis=0), iyh[...], iyl[...])
            planes = [part_rows(lines[i * Z : (i + 1) * Z]) for i in range(len(values))]
            return table_dot(izh[...], izl[...], jnp.concatenate(planes, axis=1))

        last = back([last_values()])
        last = jnp.concatenate([last[2 * Z - SLABS :], last[: 2 * Z - SLABS]], axis=0)

        def pair_back(i, carry):
            j = 2 * i
            planes = back([slot_values(j), slot_values(j + 1)])
            keep = jnp.where(first_part, 1.0, jnp.where(s + j == 0, 0.0, 1.0))
            values = (planes[:, :128] * keep + last * (1.0 - keep), planes[:, 128:])
            for k in range(2):
                for d in range(SPACE):
                    send_i[n, rows_of(d * MSG + (j + k) * 8, 8), :] = values[k][8 * d : 8 * d + 8]
            return carry

        source, target, send_sem, recv_sem = send_i.at[n], recv_i.at[n], inv_send.at[n], inv_recv.at[n]

        def part_back(q, carry):
            lax.fori_loop(q * PAIRS, (q + 1) * PAIRS, pair_back, 0)
            exchange_part(source, target, send_sem, recv_sem, q)
            return carry

        lax.fori_loop(0, NQ, part_back, 0)

        def part_wait(q, carry):
            wait_part(source, target, send_sem, recv_sem, q)
            return carry

        lax.fori_loop(0, NQ, part_wait, 0)

    def cells(n, z):
        columns = []
        for i in range(2):
            parts = [
                recv_i[n, pl.ds(part * SLABS + z + i, X // 2, stride=8), :] for part in range(2)
            ]
            columns.append(jnp.concatenate(parts, axis=0))
        return table_dot(ixh[...], ixl[...], jnp.concatenate(columns, axis=1))

    lane = lax.broadcasted_iota(jnp.int32, (1, 128), 1)

    def centroid(it):
        top = jnp.full((8, 128), -jnp.inf, F32)
        for z in range(0, SLABS, 2):
            value = cells(it, z) * SHARPNESS
            for i in range(2):
                plane = value[:, i * 128 : (i + 1) * 128]
                scores[z + i] = plane
                top = jnp.maximum(top, jnp.max(plane.reshape(X // 8, 8, 128), axis=0))
        top = jnp.max(jnp.max(top, axis=0, keepdims=True), axis=1, keepdims=True)
        step = 128
        x_row = lax.broadcasted_iota(jnp.int32, (step, 128), 0)
        zero = jnp.zeros((8, 128), F32)

        def weigh(i, carry):
            total, by_z, by_x = carry
            z, x = i // (X // step), (i % (X // step)) * step
            weights = jnp.exp(scores[z, rows_of(x, step), :] - top)
            x_at = ((x + x_row + X // 2) % X - X // 2).astype(F32)
            z_at = ((s * SLABS + z + Z // 2) % Z - Z // 2).astype(F32)
            here = jnp.sum(weights.reshape(step // 8, 8, 128), axis=0)
            by_x = by_x + jnp.sum((weights * x_at).reshape(step // 8, 8, 128), axis=0)
            return total + here, by_z + here * z_at, by_x

        total, by_z, by_x = lax.fori_loop(0, SLABS * X // step, weigh, (zero, zero, zero))
        y_at = ((lane + Y // 2) % Y - Y // 2).astype(F32)
        sums = [jnp.sum(value, axis=0, keepdims=True) for value in (total, by_z, by_x)]
        rows = [jnp.broadcast_to(top, (1, 128))] + sums + [sums[0] * y_at, jnp.zeros((3, 128), F32)]
        tile = jnp.concatenate(rows, axis=0)
        stats_out[it] = tile
        stats_in[it, s] = tile

        def stat(i, target, sender):
            d = (s + i) % SPACE
            return pltpu.make_async_remote_copy(
                src_ref=stats_out.at[it],
                dst_ref=stats_in.at[it, s if sender else d],
                send_sem=st_send.at[it, d],
                recv_sem=st_recv.at[it, s if sender else d],
                device_id={"space": d},
                device_id_type=MESH,
            )

        def send(i, carry):
            stat(i, s, True).start()
            return carry

        def receive(i, carry):
            stat(i, s, False).wait_recv()
            return carry

        lax.fori_loop(1, SPACE, send, 0)
        lax.fori_loop(1, SPACE, receive, 0)
        every = stats_in[it]
        tops = every[:, 0:1, :]
        scale = jnp.exp(tops - jnp.max(tops, axis=0, keepdims=True))
        sums = jnp.sum(jnp.sum(every * scale, axis=0), axis=1, keepdims=True)
        return [sums[i : i + 1] / sums[1:2] for i in (2, 3, 4)]

    def make_ramp(shifts):
        by_z, by_x, by_y = shifts
        kz = lax.broadcasted_iota(jnp.int32, (Z, 128), 0)
        ky = lax.broadcasted_iota(jnp.int32, (Z, 128), 1)
        phase = (2.0 * math.pi) * (signed(kz, Z) * (by_z / Z) + signed(ky, Y) * (by_y / Y))
        ramp_zy[0] = jnp.cos(phase)
        ramp_zy[1] = jnp.sin(phase)
        kx = s * SLOTS + lax.broadcasted_iota(jnp.int32, (SLOTS, 128), 0)
        phase = (2.0 * math.pi) * (kx.astype(F32) * (by_x / X))
        cos_x, sin_x = jnp.cos(phase), jnp.sin(phase)
        for j in range(SLOTS):
            ramp_x[0, j] = jnp.broadcast_to(cos_x[j : j + 1], (8, 128))
            ramp_x[1, j] = jnp.broadcast_to(sin_x[j : j + 1], (8, 128))

    def shifted_slot(j):
        cos_x = jnp.concatenate([ramp_x[0, j]] * (Z // 8), axis=0)
        sin_x = jnp.concatenate([ramp_x[1, j]] * (Z // 8), axis=0)
        cosine = ramp_zy[0] * cos_x - ramp_zy[1] * sin_x
        sine = ramp_zy[1] * cos_x + ramp_zy[0] * sin_x
        f_re, f_im = slot_of(spec, j)
        return f_re * cosine - f_im * sine, f_re * sine + f_im * cosine

    def shifted_last():
        f_re, f_im = last_slot(spec)
        return f_re * ramp_zy[0] - f_im * ramp_zy[1], f_re * ramp_zy[1] + f_im * ramp_zy[0]

    for it in range(ITERS):
        if it > 0:

            def shift_one(j, carry):
                re, im = shifted_slot(j)
                moved[j, 0:Z, :] = re
                moved[j, Z : 2 * Z, :] = im
                return carry

            lax.fori_loop(0, SLOTS, shift_one, 0)
            value = jnp.concatenate(shifted_last(), axis=0)
            for u in range(SLOTS):
                moved[u, 2 * Z :, :] = value[8 * u : 8 * u + 8]
        template_sum(it, moved if it > 0 else spec)
        inverse(
            it,
            lambda j: whiten(*slot_of(spec, j), *slot_of(tmpl.at[it], j)),
            lambda: whiten(*last_slot(spec), *last_slot(tmpl.at[it])),
        )
        shifts = centroid(it)
        make_ramp(shifts)

    inverse(ITERS, shifted_slot, shifted_last)
    for z in range(0, SLABS, 2):
        value = cells(ITERS, z)
        for i in range(2):
            out_ref[z + i] = value[:, i * 128 : (i + 1) * 128]
    by_z, by_x, by_y = shifts
    line = jnp.where(lane == 0, by_z, jnp.where(lane == 1, by_x, by_y))
    shift_ref[...] = line[:, 0:3]

    for copy in sends:
        copy.wait_send()

    def finish(q, carry):
        wait_sent(send_f, recv_f, fwd_send, fwd_recv, q)
        for n in range(ITERS + 1):
            wait_sent(send_i.at[n], recv_i.at[n], inv_send.at[n], inv_recv.at[n], q)
        return carry

    lax.fori_loop(0, NQ, finish, 0)
    for it in range(ITERS):

        def done(i, carry):
            d = (s + i) % SPACE
            pltpu.make_async_remote_copy(
                src_ref=stats_out.at[it],
                dst_ref=stats_in.at[it, s],
                send_sem=st_send.at[it, d],
                recv_sem=st_recv.at[it, s],
                device_id={"space": d},
                device_id_type=MESH,
            ).wait_send()
            return carry

        lax.fori_loop(1, SPACE, done, 0)


def body(volumes):
    consts = [jnp.asarray(table) for table in tables()]
    vmem = pl.BlockSpec(memory_space=pltpu.VMEM)
    dma = pltpu.SemaphoreType.DMA
    corrected, shifts = pl.pallas_call(
        kernel,
        out_shape=(
            jax.ShapeDtypeStruct((SLABS, X, Y), F32),
            jax.ShapeDtypeStruct((1, 3), F32),
        ),
        in_specs=[vmem] * (1 + len(consts)),
        out_specs=(vmem, vmem),
        scratch_shapes=[
            pltpu.VMEM((ROWS, 128), F32),
            pltpu.VMEM((ROWS, 128), F32),
            pltpu.VMEM((SLOTS, UNIT, 128), F32),
            pltpu.VMEM((SLOTS, UNIT, 128), F32),
            pltpu.VMEM((ITERS, CHIPS, UNIT, 128), F32),
            pltpu.VMEM((ITERS, CHIPS, UNIT, 128), F32),
            pltpu.VMEM((ITERS, 4, UNIT, 128), F32),
            pltpu.VMEM((ITERS, 3, UNIT, 128), F32),
            pltpu.VMEM((ITERS, 4, UNIT, 128), F32),
            pltpu.VMEM((ITERS, 3, UNIT, 128), F32),
            pltpu.VMEM((ITERS, SLOTS, UNIT, 128), F32),
            pltpu.VMEM((ITERS + 1, ROWS, 128), F32),
            pltpu.VMEM((ITERS + 1, ROWS, 128), F32),
            pltpu.VMEM((SLABS, X, 128), F32),
            pltpu.VMEM((ITERS, 8, 128), F32),
            pltpu.VMEM((ITERS, SPACE, 8, 128), F32),
            pltpu.VMEM((2, Z, 128), F32),
            pltpu.VMEM((2, SLOTS, 8, 128), F32),
            dma((NQ, SPACE)), dma((NQ, SPACE)),
            dma((ITERS + 1, NQ, SPACE)), dma((ITERS + 1, NQ, SPACE)),
            dma((ITERS, SPACE)), dma((ITERS, SPACE)),
            dma((ITERS,)), dma((ITERS,)),
            dma((ITERS, 4)), dma((ITERS, 4)),
            dma((ITERS, 3)), dma((ITERS, 3)),
            dma((ITERS, 4)), dma((ITERS, 4)),
            dma((ITERS, 3)), dma((ITERS, 3)),
            dma((ITERS, CHIPS)), dma((ITERS, CHIPS)),
        ],
        compiler_params=pltpu.CompilerParams(
            collective_id=0, has_side_effects=True, vmem_limit_bytes=50 * 2**20
        ),
        name="register",
    )(volumes[0], *consts)
    return corrected[None], shifts


def solution(mesh):
    in_specs = (P("tm", "space", None, None),)
    out_specs = (P("tm", "space", None, None), P("tm", None))
    return jax.shard_map(body, mesh=mesh, in_specs=in_specs, out_specs=out_specs, check_vma=False)
```

time: 724 us -> 172 us (0.24)
  the two profiles are of different devices: /device:TPU:96 before, /device:TPU:1 now
where the time goes in v1:
time: 172 us
  Pallas kernels  159 us (92%)
  local copies, waits for them, and re-layouts  12.3 us (7%)
    pallas_call x1, Pallas kernels, body(): pl.pallas_call(kernel, out_shape=(jax.ShapeDtypeStruct((SLABS, X, Y), F32...  159 us
    unnamed x26, local copies, waits for them, and re-layouts  12.3 us

profile of v1, /device:TPU:1, one launch (start us, length us, event | category | flops | bytes accessed | tf_op | source)
XLA Modules:
  0.0 171.6 jit_solution(2853848859758811655)
XLA Ops:
  0.6 0.0 copy-start
  0.6 1.0 copy-done
  1.7 0.0 copy-start.1
  1.7 1.0 copy-done.1
  2.7 0.0 copy-start.2
  2.7 1.0 copy-done.2
  3.8 0.0 copy-start.3
  3.8 1.0 copy-done.3
  4.8 0.0 copy-start.4
  4.8 0.9 copy-done.4
  5.7 0.0 copy-start.5
  5.7 0.9 copy-done.5
  6.6 0.0 copy-start.6
  6.6 0.9 copy-done.6
  7.5 0.0 copy-start.7
  7.5 0.9 copy-done.7
  8.4 0.0 copy-start.8
  8.4 0.8 copy-done.8
  9.2 0.0 copy-start.9
  9.2 0.8 copy-done.9
  9.9 0.0 copy-start.10
  9.9 0.8 copy-done.10
  10.7 0.0 copy-start.11
  10.7 0.8 copy-done.11
  11.5 158.7 %register.1 = (f32[4,512,128]{2,1,0:T(8,128)S(1)}, f32[1,3]{1,0:T(1,128)S(1)}) custom-call(f32[4,512,128]{2,1,0:T(8,128)} %bitcast.3, bf16[512,512]{1,0:T(8,128)(2,1)S(1)} %copy-done.3, bf16[512,512]{1,0:T(8,128)(2,1)S(1)} %copy-done.2, bf16[512,512]{1,0:T(8,128)(2,1)S(1)} %copy-done.1, bf16[512,512]{1,0:T(8,128)(2,1)S(1)} %copy-done, ...), custom_call_target="tpu_custom_call" | custom-call | tf_op jit(solution)/shard_map/register/pallas_call | solution.py:513
  170.1 1.0 copy.17
  171.1 0.5 copy.18
Async XLA Ops:
  0.6 1.0 copy-start
  1.7 1.0 copy-start.1
  2.7 1.0 copy-start.2
  3.8 1.0 copy-start.3
  4.8 0.9 copy-start.4
  5.7 0.9 copy-start.5
  6.6 0.9 copy-start.6
  7.5 0.9 copy-start.7
  8.4 0.8 copy-start.8
  9.2 0.8 copy-start.9
  9.9 0.8 copy-start.10
  10.7 0.8 copy-start.11

commit v2 on v1

--- a/solution.py
+++ b/solution.py
@@ -24,9 +24,10 @@
 SLOTS = X // 2 // SPACE
 ROWS = SPACE * SLOTS * 8
 MSG = SLOTS * 8
-UNIT = 2 * Z + 8
 NQ = 4
 PART = MSG // NQ
+HALF = SLOTS // NQ * Z
+UNIT = HALF // CHIPS
 PAIRS = SLOTS // 2 // NQ
 MESH = pl.DeviceIdType.MESH
 F32 = jnp.float32
@@ -65,8 +66,11 @@
     for table in (forward_x, inverse_x, forward_y, inverse_y, forward_z, inverse_z):
         high = table.astype(np.float32).astype(ml_dtypes.bfloat16)
         low = (table - high.astype(np.float64)).astype(np.float32).astype(ml_dtypes.bfloat16)
-        out += [high, low]
-    return out
+        out.append(np.stack([high, low]))
+    flips = [np.zeros((n, n), ml_dtypes.bfloat16) for n in (Z, Y)]
+    for flip in flips:
+        flip[np.arange(len(flip)), -np.arange(len(flip))] = 1.0
+    return out + flips
 
 
 def split(value):
@@ -78,14 +82,14 @@
     return jnp.dot(a, b, preferred_element_type=F32)
 
 
-def table_dot(high, low, data):
+def table_dot(table, data):
     data_high, data_low = split(data)
-    return dot(high, data_high) + (dot(high, data_low) + dot(low, data_high))
-
-
-def dot_table(data, high, low):
+    return dot(table[0], data_high) + (dot(table[0], data_low) + dot(table[1], data_high))
+
+
+def dot_table(data, table):
     data_high, data_low = split(data)
-    return dot(data_high, high) + (dot(data_low, high) + dot(data_high, low))
+    return dot(data_high, table[0]) + (dot(data_low, table[0]) + dot(data_high, table[1]))
 
 
 def rows_of(start, count):
@@ -98,11 +102,13 @@
 
 
 def kernel(
-    v_ref, fxh, fxl, ixh, ixl, fyh, fyl, iyh, iyl, fzh, fzl, izh, izl,
+    v_hbm, fx_hbm, ix_hbm, fy_hbm, iy_hbm, fz_hbm, iz_hbm, flip_z_hbm, flip_y_hbm,
     out_ref, shift_ref,
-    send_f, recv_f, spec, moved, other, pair, ring_r, ring_l, sent_r, sent_l, tmpl,
+    v_ref, fx, ix, fy, iy, fz, iz, flip_z, flip_y,
+    send_f, recv_f, spec, moved, first_f, last_f, first_t, last_t, other, pair,
+    ring_r, ring_l, sent_r, sent_l, tmpl,
     send_i, recv_i, scores, stats_out, stats_in, ramp_zy, ramp_x,
-    fwd_send, fwd_recv, inv_send, inv_recv, st_send, st_recv,
+    load_sem, fwd_send, fwd_recv, inv_send, inv_recv, st_send, st_recv,
     oc_send, oc_recv, rr_send, rr_recv, rl_send, rl_recv,
     gr_send, gr_recv, gl_send, gl_recv, go_send, go_recv,
 ):
@@ -114,6 +120,18 @@
     right = ((chip + 1) % CHIPS) * 2 + core
     left = ((chip + CHIPS - 1) % CHIPS) * 2 + core
 
+    loads = [
+        pltpu.make_async_copy(source, target, load_sem.at[i])
+        for i, (source, target) in enumerate(
+            [
+                (fx_hbm, fx), (v_hbm, v_ref), (fz_hbm, fz), (fy_hbm, fy), (iy_hbm, iy),
+                (iz_hbm, iz), (flip_z_hbm, flip_z), (flip_y_hbm, flip_y), (ix_hbm, ix),
+            ]
+        )
+    ]
+    for copy in loads:
+        copy.start()
+
     barrier = pltpu.get_barrier_semaphore()
 
     def greet(i, carry):
@@ -137,9 +155,12 @@
             device_id_type=MESH,
         )
 
+    for copy in loads[:2]:
+        copy.wait()
+
     for z in range(0, SLABS, 2):
         data = jnp.concatenate([v_ref[z], v_ref[z + 1]], axis=1)
-        result = table_dot(fxh[...], fxl[...], data)
+        result = table_dot(fx, data)
         for i in range(2):
             for part in range(2):
                 send_f[pl.ds(part * SLABS + z + i, X // 2, stride=8), :] = result[
@@ -188,6 +209,8 @@
         return carry
 
     lax.fori_loop(0, NQ, send_all, 0)
+    for copy in loads[2:]:
+        copy.wait()
 
     def load_slot(j):
         return jnp.concatenate([recv_f[rows_of(d * MSG + j * 8, 8), :] for d in range(SPACE)], axis=0)
@@ -198,32 +221,33 @@
     def part_rows(value):
         return jnp.concatenate([value[:, :128], value[:, 128:]], axis=0)
 
+    def spectrum_two(a, b):
+        zed = table_dot(fz, jnp.concatenate([a, b], axis=1))
+        lines = jnp.concatenate([complex_rows(zed[:, :128]), complex_rows(zed[:, 128:])], axis=0)
+        freq = dot_table(lines, fy)
+        return part_rows(freq[:Z]), part_rows(freq[Z:])
+
+    def slot_rows(j):
+        return rows_of(j * 2 * Z, 2 * Z)
+
     def spectrum_pair(i, carry):
         j = 2 * i
-        keep = jnp.where(first_part, 1.0, jnp.where(s + j == 0, 0.0, 1.0))
-        data = jnp.concatenate([load_slot(j) * keep, load_slot(j + 1)], axis=1)
-        zed = table_dot(fzh[...], fzl[...], data)
-        lines = jnp.concatenate([complex_rows(zed[:, :128]), complex_rows(zed[:, 128:])], axis=0)
-        freq = dot_table(lines, fyh[...], fyl[...])
-        spec[j, 0 : 2 * Z, :] = part_rows(freq[:Z])
-        spec[j + 1, 0 : 2 * Z, :] = part_rows(freq[Z:])
+        a, b = spectrum_two(load_slot(j), load_slot(j + 1))
+        spec[slot_rows(j), :] = a
+        spec[slot_rows(j + 1), :] = b
         return carry
 
-    def forward_part(q, carry):
+    owner = jnp.where(s == 0, 1.0, 0.0)
+
+    def forward_part(q):
         wait_part(send_f, recv_f, fwd_send, fwd_recv, q)
-        return lax.fori_loop(q * PAIRS, (q + 1) * PAIRS, spectrum_pair, carry)
-
-    lax.fori_loop(0, NQ, forward_part, 0)
-
-    slot = load_slot(0)
-    slot = jnp.concatenate([slot[SLABS:], slot[:SLABS]], axis=0)
-    slot = slot * jnp.where(first_part, jnp.where(s == 0, 1.0, 0.0), 0.0)
-    freq = dot_table(complex_rows(table_dot(fzh[...], fzl[...], slot)), fyh[...], fyl[...])
-    freq = part_rows(freq)
-    for u in range(SLOTS):
-        spec[u, 2 * Z :, :] = freq[8 * u : 8 * u + 8]
-
-    base = core * CHIPS
+        lax.fori_loop(q * PAIRS, (q + 1) * PAIRS, spectrum_pair, 0)
+        if q == 0:
+            slot = load_slot(0)
+            keep = jnp.where(first_part, 1.0, 1.0 - owner)
+            rolled = jnp.concatenate([slot[SLABS:], slot[:SLABS]], axis=0)
+            first_f[...], last_f[...] = spectrum_two(slot * keep, rolled * jnp.where(first_part, owner, 0.0))
+
     sends = []
 
     def to_tm(source, target, send_sem, recv_sem, device):
@@ -240,70 +264,89 @@
         copy.start()
         sends.append(copy)
 
-    def template_sum(it, source):
-        copy = to_tm(
-            source.at[pl.ds((1 - core) * CHIPS, CHIPS)], other.at[it], oc_send.at[it], oc_recv.at[it], mate
+    def half_rows(q, c):
+        return rows_of((2 * q + c) * HALF, HALF)
+
+    def sum_steps(it, q, source):
+        def pair_unit(i):
+            return pair.at[it, q, rows_of((i % CHIPS) * UNIT, UNIT)]
+
+        def mean_unit(i):
+            return tmpl.at[it, rows_of((2 * q + core) * HALF + (i % CHIPS) * UNIT, UNIT)]
+
+        def swap():
+            return to_tm(source.at[half_rows(q, 1 - core)], other.at[it, q], oc_send.at[it, q], oc_recv.at[it, q], mate)
+
+        def sum_r(outgoing, k):
+            return to_tm(outgoing, ring_r.at[it, q, k], rr_send.at[it, q, k], rr_recv.at[it, q, k], right)
+
+        def sum_l(outgoing, k):
+            return to_tm(outgoing, ring_l.at[it, q, k], rl_send.at[it, q, k], rl_recv.at[it, q, k], left)
+
+        def mean_r(i, k):
+            return to_tm(mean_unit(i), mean_unit(i), gr_send.at[it, q, k], gr_recv.at[it, q, k], right)
+
+        def mean_l(i, k):
+            return to_tm(mean_unit(i), mean_unit(i), gl_send.at[it, q, k], gl_recv.at[it, q, k], left)
+
+        def to_mate(c):
+            ref = tmpl.at[it, half_rows(q, c)]
+            return to_tm(ref, ref, go_send.at[it, q], go_recv.at[it, q], mate)
+
+        def step_swap():
+            start(swap())
+
+        def step_pair():
+            swap().wait_recv()
+            pair[it, q] = source[half_rows(q, core), :] + other[it, q]
+            start(sum_r(pair_unit(chip + 4), 0))
+            start(sum_l(pair_unit(chip + CHIPS - 3), 0))
+
+        def step_sum(k):
+            def run():
+                sum_r(sent_r.at[it, q, k - 1], k - 1).wait_recv()
+                sent_r[it, q, k - 1] = pair_unit(chip + 4 - k)[...] + ring_r[it, q, k - 1]
+                start(sum_r(sent_r.at[it, q, k - 1], k))
+                if k < 3:
+                    sum_l(sent_l.at[it, q, k - 1], k - 1).wait_recv()
+                    sent_l[it, q, k - 1] = pair_unit(chip + CHIPS - 3 + k)[...] + ring_l[it, q, k - 1]
+                    start(sum_l(sent_l.at[it, q, k - 1], k))
+
+            return run
+
+        def step_mean():
+            sum_l(ring_l.at[it, q, 2], 2).wait_recv()
+            sum_r(ring_r.at[it, q, 3], 3).wait_recv()
+            total = pair_unit(chip)[...] + (ring_r[it, q, 3] + ring_l[it, q, 2])
+            tmpl[it, rows_of((2 * q + core) * HALF + chip * UNIT, UNIT), :] = total * (1.0 / FRAMES)
+            start(mean_r(chip, 0))
+            start(mean_l(chip, 0))
+
+        def step_pass(k):
+            def run():
+                mean_r(chip + CHIPS - k, k - 1).wait_recv()
+                start(mean_r(chip + CHIPS - k, k))
+                if k < 3:
+                    mean_l(chip + k, k - 1).wait_recv()
+                    start(mean_l(chip + k, k))
+
+            return run
+
+        def step_share():
+            mean_l(chip + 3, 2).wait_recv()
+            mean_r(chip + 4, 3).wait_recv()
+            start(to_mate(core))
+
+        def step_end():
+            to_mate(1 - core).wait_recv()
+
+        return (
+            [step_swap, step_pair]
+            + [step_sum(k) for k in (1, 2, 3)]
+            + [step_mean]
+            + [step_pass(k) for k in (1, 2, 3)]
+            + [step_share, step_end]
         )
-        start(copy)
-        copy.wait_recv()
-
-        def add(u, carry):
-            pair[it, u] = source[base + u] + other[it, u]
-            return carry
-
-        lax.fori_loop(0, CHIPS, add, 0)
-        for k in range(4):
-            unit = (chip + 4 - k) % CHIPS
-            if k == 0:
-                outgoing = pair.at[it, unit]
-            else:
-                to_tm(sent_r.at[it, k], ring_r.at[it, k - 1], rr_send.at[it, k - 1], rr_recv.at[it, k - 1], left).wait_recv()
-                sent_r[it, k] = pair[it, unit] + ring_r[it, k - 1]
-                outgoing = sent_r.at[it, k]
-            start(to_tm(outgoing, ring_r.at[it, k], rr_send.at[it, k], rr_recv.at[it, k], right))
-            if k < 3:
-                unit = (chip + CHIPS - 3 + k) % CHIPS
-                if k == 0:
-                    outgoing = pair.at[it, unit]
-                else:
-                    to_tm(sent_l.at[it, k], ring_l.at[it, k - 1], rl_send.at[it, k - 1], rl_recv.at[it, k - 1], right).wait_recv()
-                    sent_l[it, k] = pair[it, unit] + ring_l[it, k - 1]
-                    outgoing = sent_l.at[it, k]
-                start(to_tm(outgoing, ring_l.at[it, k], rl_send.at[it, k], rl_recv.at[it, k], left))
-        to_tm(ring_r.at[it, 3], ring_r.at[it, 3], rr_send.at[it, 3], rr_recv.at[it, 3], left).wait_recv()
-        to_tm(ring_l.at[it, 2], ring_l.at[it, 2], rl_send.at[it, 2], rl_recv.at[it, 2], right).wait_recv()
-        tmpl[it, base + chip] = (pair[it, chip] + (ring_r[it, 3] + ring_l[it, 2])) * (1.0 / FRAMES)
-
-        def to_mate(unit):
-            ref = tmpl.at[it, base + unit]
-            start(to_tm(ref, ref, go_send.at[it, unit], go_recv.at[it, unit], mate))
-
-        for k in range(4):
-            unit = (chip + CHIPS - k) % CHIPS
-            ref = tmpl.at[it, base + unit]
-            if k > 0:
-                to_tm(ref, ref, gr_send.at[it, k - 1], gr_recv.at[it, k - 1], left).wait_recv()
-            start(to_tm(ref, ref, gr_send.at[it, k], gr_recv.at[it, k], right))
-            if k < 3:
-                unit_l = (chip + k) % CHIPS
-                ref_l = tmpl.at[it, base + unit_l]
-                if k > 0:
-                    to_tm(ref_l, ref_l, gl_send.at[it, k - 1], gl_recv.at[it, k - 1], right).wait_recv()
-                start(to_tm(ref_l, ref_l, gl_send.at[it, k], gl_recv.at[it, k], left))
-                if k > 0:
-                    to_mate(unit_l)
-            to_mate(unit)
-        unit = (chip + 4) % CHIPS
-        ref = tmpl.at[it, base + unit]
-        to_tm(ref, ref, gr_send.at[it, 3], gr_recv.at[it, 3], left).wait_recv()
-        to_mate(unit)
-        unit = (chip + 3) % CHIPS
-        ref = tmpl.at[it, base + unit]
-        to_tm(ref, ref, gl_send.at[it, 2], gl_recv.at[it, 2], right).wait_recv()
-        to_mate(unit)
-        for u in range(CHIPS):
-            ref = tmpl.at[it, (1 - core) * CHIPS + u]
-            to_tm(ref, ref, go_send.at[it, u], go_recv.at[it, u], mate).wait_recv()
 
     def whiten(f_re, f_im, t_re, t_im):
         p_re = f_re * t_re + f_im * t_im
@@ -311,47 +354,62 @@
         scale = lax.rsqrt(jnp.maximum(p_re * p_re + p_im * p_im, FLOOR * FLOOR))
         return p_re * scale, p_im * scale
 
-    def slot_of(ref, j):
-        return ref[j, 0:Z, :], ref[j, Z : 2 * Z, :]
-
-    def last_slot(ref):
-        value = jnp.concatenate([ref[u, 2 * Z :, :] for u in range(SLOTS)], axis=0)
+    def halves(value):
         return value[:Z], value[Z:]
 
-    def inverse(n, slot_values, last_values):
-        def back(values):
-            lines = [jnp.concatenate([re, im], axis=1) for re, im in values]
-            lines = dot_table(jnp.concatenate(lines, axis=0), iyh[...], iyl[...])
-            planes = [part_rows(lines[i * Z : (i + 1) * Z]) for i in range(len(values))]
-            return table_dot(izh[...], izl[...], jnp.concatenate(planes, axis=1))
-
-        last = back([last_values()])
-        last = jnp.concatenate([last[2 * Z - SLABS :], last[: 2 * Z - SLABS]], axis=0)
+    def slot_of(ref, first, j):
+        return halves(jnp.where(j == 0, first[...], ref[slot_rows(j), :]))
+
+    def packed(first, last):
+        (f_re, f_im), (l_re, l_im) = first, last
+        return jnp.concatenate([f_re - l_im, f_im + l_re], axis=0)
+
+    def flipped(value):
+        high, low = split(value)
+        value = dot(flip_z[...], high) + dot(flip_z[...], low)
+        high, low = split(part_rows(value))
+        return halves(dot(high, flip_y[...]) + dot(low, flip_y[...]))
+
+    def unpack(it):
+        value = tmpl[it, slot_rows(0), :]
+        re, im = halves(value)
+        flip_re, flip_im = flipped(complex_rows(value))
+        half = 0.5 * owner
+        first_t[it] = jnp.concatenate([re - half * (re - flip_re), im - half * (im + flip_im)], axis=0)
+        last_t[it] = jnp.concatenate([half * (im + flip_im), half * (flip_re - re)], axis=0)
+
+    def back(values):
+        lines = [jnp.concatenate([re, im], axis=1) for re, im in values]
+        lines = dot_table(jnp.concatenate(lines, axis=0), iy)
+        planes = [part_rows(lines[i * Z : (i + 1) * Z]) for i in range(len(values))]
+        return table_dot(iz, jnp.concatenate(planes, axis=1))
+
+    def inverse_part(n, q, slot_values, last_values):
+        if q == 0:
+            last = back([last_values()])
+            last = jnp.concatenate([last[2 * Z - SLABS :], last[: 2 * Z - SLABS]], axis=0)
 
         def pair_back(i, carry):
             j = 2 * i
             planes = back([slot_values(j), slot_values(j + 1)])
-            keep = jnp.where(first_part, 1.0, jnp.where(s + j == 0, 0.0, 1.0))
-            values = (planes[:, :128] * keep + last * (1.0 - keep), planes[:, 128:])
+            values = [planes[:, :128], planes[:, 128:]]
+            if q == 0:
+                keep = jnp.where(first_part, 1.0, jnp.where(s + j == 0, 0.0, 1.0))
+                values[0] = values[0] * keep + last * (1.0 - keep)
             for k in range(2):
                 for d in range(SPACE):
                     send_i[n, rows_of(d * MSG + (j + k) * 8, 8), :] = values[k][8 * d : 8 * d + 8]
             return carry
 
-        source, target, send_sem, recv_sem = send_i.at[n], recv_i.at[n], inv_send.at[n], inv_recv.at[n]
-
-        def part_back(q, carry):
-            lax.fori_loop(q * PAIRS, (q + 1) * PAIRS, pair_back, 0)
-            exchange_part(source, target, send_sem, recv_sem, q)
-            return carry
-
-        lax.fori_loop(0, NQ, part_back, 0)
-
-        def part_wait(q, carry):
-            wait_part(source, target, send_sem, recv_sem, q)
-            return carry
-
-        lax.fori_loop(0, NQ, part_wait, 0)
+        lax.fori_loop(q * PAIRS, (q + 1) * PAIRS, pair_back, 0)
+        exchange_part(send_i.at[n], recv_i.at[n], inv_send.at[n], inv_recv.at[n], q)
+
+    def inverse_wait(n):
+        def one(q, carry):
+            wait_part(send_i.at[n], recv_i.at[n], inv_send.at[n], inv_recv.at[n], q)
+            return carry
+
+        lax.fori_loop(0, NQ, one, 0)
 
     def cells(n, z):
         columns = []
@@ -360,7 +418,7 @@
                 recv_i[n, pl.ds(part * SLABS + z + i, X // 2, stride=8), :] for part in range(2)
             ]
             columns.append(jnp.concatenate(parts, axis=0))
-        return table_dot(ixh[...], ixl[...], jnp.concatenate(columns, axis=1))
+        return table_dot(ix, jnp.concatenate(columns, axis=1))
 
     lane = lax.broadcasted_iota(jnp.int32, (1, 128), 1)
 
@@ -441,36 +499,56 @@
         sin_x = jnp.concatenate([ramp_x[1, j]] * (Z // 8), axis=0)
         cosine = ramp_zy[0] * cos_x - ramp_zy[1] * sin_x
         sine = ramp_zy[1] * cos_x + ramp_zy[0] * sin_x
-        f_re, f_im = slot_of(spec, j)
+        f_re, f_im = slot_of(spec, first_f, j)
         return f_re * cosine - f_im * sine, f_re * sine + f_im * cosine
 
     def shifted_last():
-        f_re, f_im = last_slot(spec)
+        f_re, f_im = halves(last_f[...])
         return f_re * ramp_zy[0] - f_im * ramp_zy[1], f_re * ramp_zy[1] + f_im * ramp_zy[0]
 
+    def shift_one(j, carry):
+        moved[slot_rows(j), :] = jnp.concatenate(shifted_slot(j), axis=0)
+        return carry
+
+    def shift_part(q):
+        lax.fori_loop(q * 2 * PAIRS, (q + 1) * 2 * PAIRS, shift_one, 0)
+        if q == 0:
+            moved[slot_rows(0), :] = packed(halves(moved[slot_rows(0), :]), shifted_last())
+
     for it in range(ITERS):
-        if it > 0:
-
-            def shift_one(j, carry):
-                re, im = shifted_slot(j)
-                moved[j, 0:Z, :] = re
-                moved[j, Z : 2 * Z, :] = im
-                return carry
-
-            lax.fori_loop(0, SLOTS, shift_one, 0)
-            value = jnp.concatenate(shifted_last(), axis=0)
-            for u in range(SLOTS):
-                moved[u, 2 * Z :, :] = value[8 * u : 8 * u + 8]
-        template_sum(it, moved if it > 0 else spec)
-        inverse(
-            it,
-            lambda j: whiten(*slot_of(spec, j), *slot_of(tmpl.at[it], j)),
-            lambda: whiten(*last_slot(spec), *last_slot(tmpl.at[it])),
-        )
+
+        def part_steps(q):
+            def begin():
+                if it == 0:
+                    forward_part(q)
+                else:
+                    shift_part(q)
+
+            def end():
+                if q == 0:
+                    unpack(it)
+                inverse_part(
+                    it,
+                    q,
+                    lambda j: whiten(*slot_of(spec, first_f, j), *slot_of(tmpl.at[it], first_t.at[it], j)),
+                    lambda: whiten(*halves(last_f[...]), *halves(last_t[it])),
+                )
+
+            steps = sum_steps(it, q, moved if it > 0 else spec)
+            return [lambda: (begin(), steps[0]())] + steps[1:-1] + [lambda: (steps[-1](), end())]
+
+        plan = [part_steps(q) for q in range(NQ)]
+        for wave in range(NQ + len(plan[0]) - 1):
+            for q in range(NQ):
+                if 0 <= wave - q < len(plan[q]):
+                    plan[q][wave - q]()
+        inverse_wait(it)
         shifts = centroid(it)
         make_ramp(shifts)
 
-    inverse(ITERS, shifted_slot, shifted_last)
+    for q in range(NQ):
+        inverse_part(ITERS, q, shifted_slot, shifted_last)
+    inverse_wait(ITERS)
     for z in range(0, SLABS, 2):
         value = cells(ITERS, z)
         for i in range(2):
@@ -509,27 +587,35 @@
 def body(volumes):
     consts = [jnp.asarray(table) for table in tables()]
     vmem = pl.BlockSpec(memory_space=pltpu.VMEM)
+    hbm = pl.BlockSpec(memory_space=pltpu.HBM)
     dma = pltpu.SemaphoreType.DMA
+    slots = SLOTS * 2 * Z
     corrected, shifts = pl.pallas_call(
         kernel,
         out_shape=(
             jax.ShapeDtypeStruct((SLABS, X, Y), F32),
             jax.ShapeDtypeStruct((1, 3), F32),
         ),
-        in_specs=[vmem] * (1 + len(consts)),
+        in_specs=[hbm] * (1 + len(consts)),
         out_specs=(vmem, vmem),
         scratch_shapes=[
+            pltpu.VMEM((SLABS, X, Y), F32),
+            *[pltpu.VMEM(table.shape, BF16) for table in consts],
             pltpu.VMEM((ROWS, 128), F32),
             pltpu.VMEM((ROWS, 128), F32),
-            pltpu.VMEM((SLOTS, UNIT, 128), F32),
-            pltpu.VMEM((SLOTS, UNIT, 128), F32),
-            pltpu.VMEM((ITERS, CHIPS, UNIT, 128), F32),
-            pltpu.VMEM((ITERS, CHIPS, UNIT, 128), F32),
-            pltpu.VMEM((ITERS, 4, UNIT, 128), F32),
-            pltpu.VMEM((ITERS, 3, UNIT, 128), F32),
-            pltpu.VMEM((ITERS, 4, UNIT, 128), F32),
-            pltpu.VMEM((ITERS, 3, UNIT, 128), F32),
-            pltpu.VMEM((ITERS, SLOTS, UNIT, 128), F32),
+            pltpu.VMEM((slots, 128), F32),
+            pltpu.VMEM((slots, 128), F32),
+            pltpu.VMEM((2 * Z, 128), F32),
+            pltpu.VMEM((2 * Z, 128), F32),
+            pltpu.VMEM((ITERS, 2 * Z, 128), F32),
+            pltpu.VMEM((ITERS, 2 * Z, 128), F32),
+            pltpu.VMEM((ITERS, NQ, HALF, 128), F32),
+            pltpu.VMEM((ITERS, NQ, HALF, 128), F32),
+            pltpu.VMEM((ITERS, NQ, 4, UNIT, 128), F32),
+            pltpu.VMEM((ITERS, NQ, 3, UNIT, 128), F32),
+            pltpu.VMEM((ITERS, NQ, 3, UNIT, 128), F32),
+            pltpu.VMEM((ITERS, NQ, 2, UNIT, 128), F32),
+            pltpu.VMEM((ITERS, slots, 128), F32),
             pltpu.VMEM((ITERS + 1, ROWS, 128), F32),
             pltpu.VMEM((ITERS + 1, ROWS, 128), F32),
             pltpu.VMEM((SLABS, X, 128), F32),
@@ -537,18 +623,19 @@
             pltpu.VMEM((ITERS, SPACE, 8, 128), F32),
             pltpu.VMEM((2, Z, 128), F32),
             pltpu.VMEM((2, SLOTS, 8, 128), F32),
+            dma((1 + len(consts),)),
             dma((NQ, SPACE)), dma((NQ, SPACE)),
             dma((ITERS + 1, NQ, SPACE)), dma((ITERS + 1, NQ, SPACE)),
             dma((ITERS, SPACE)), dma((ITERS, SPACE)),
-            dma((ITERS,)), dma((ITERS,)),
-            dma((ITERS, 4)), dma((ITERS, 4)),
-            dma((ITERS, 3)), dma((ITERS, 3)),
-            dma((ITERS, 4)), dma((ITERS, 4)),
-            dma((ITERS, 3)), dma((ITERS, 3)),
-            dma((ITERS, CHIPS)), dma((ITERS, CHIPS)),
+            dma((ITERS, NQ)), dma((ITERS, NQ)),
+            dma((ITERS, NQ, 4)), dma((ITERS, NQ, 4)),
+            dma((ITERS, NQ, 3)), dma((ITERS, NQ, 3)),
+            dma((ITERS, NQ, 4)), dma((ITERS, NQ, 4)),
+            dma((ITERS, NQ, 3)), dma((ITERS, NQ, 3)),
+            dma((ITERS, NQ)), dma((ITERS, NQ)),
         ],
         compiler_params=pltpu.CompilerParams(
-            collective_id=0, has_side_effects=True, vmem_limit_bytes=50 * 2**20
+            collective_id=0, has_side_effects=True, vmem_limit_bytes=56 * 2**20
         ),
         name="register",
     )(volumes[0], *consts)

time: 172 us -> 149 us (0.87)
  Pallas kernels: 159 us -> 146 us
  local copies, waits for them, and re-layouts: 12.3 us -> 2.78 us
    pallas_call x1, Pallas kernels: 159 us -> 146 us  [body(): pl.pallas_call(kernel, out_shape=(jax.ShapeDtypeStruct((SLABS, X, Y), F32...]
    unnamed x26 -> x4, local copies, waits for them, and re-layouts: 12.3 us -> 2.78 us
where the time goes in v2:
time: 149 us
  Pallas kernels  146 us (98%)
  local copies, waits for them, and re-layouts  2.78 us (2%)
    pallas_call x1, Pallas kernels, body(): pl.pallas_call(kernel, out_shape=(jax.ShapeDtypeStruct((SLABS, X, Y), F32...  146 us

profile of v2, /device:TPU:1, one launch (start us, length us, event | category | flops | bytes accessed | tf_op | source)
XLA Modules:
  0.0 149.2 jit_solution(18105061654015277498)
XLA Ops:
  0.6 145.8 %register.1 = (f32[4,512,128]{2,1,0:T(8,128)}, f32[1,3]{1,0:T(1,128)}) custom-call(f32[4,512,128]{2,1,0:T(8,128)} %bitcast.3, bf16[2,512,512]{2,1,0:T(8,128)(2,1)} %constant.16.clone.fx_hbm, bf16[2,512,512]{2,1,0:T(8,128)(2,1)} %constant.17.clone.ix_hbm, bf16[2,256,256]{2,1,0:T(8,128)(2,1)} %constant.18.clone.fy_hbm, ...), custom_call_target="tpu_custom_call" | custom-call | tf_op jit(solution)/shard_map/register/pallas_call | solution.py:593
  146.5 0.0 copy-start
  146.5 2.3 %copy.13 = f32[1,4,512,128]{3,2,1,0:T(8,128)} copy(f32[1,4,512,128]{3,2,1,0:T(8,128)} %bitcast.2) | data formatting | bytes 2097152
  148.7 0.0 copy-done
  148.7 0.5 copy.14
Async XLA Ops:
  146.5 2.3 %copy-start = (f32[1,3]{1,0:T(1,128)S(1)}, f32[1,3]{1,0:T(1,128)}, u32[]{:S(2)}) copy-start(f32[1,3]{1,0:T(1,128)} %get-tuple-element.9) | copy-start | bytes 40

commit v3 on v2

--- a/solution.py
+++ b/solution.py
@@ -29,6 +29,12 @@
 HALF = SLOTS // NQ * Z
 UNIT = HALF // CHIPS
 PAIRS = SLOTS // 2 // NQ
+FIRST_SUMS = ((2, 1), (4, 1), (-3, -1), (-1, -1))
+MERGED = (1, 3, -2)
+MEANS = (-1, -3, 2, 1)
+PASSED = ((1, -1), (3, -1), (-2, 1))
+LAST_MEANS = (-1, 2, 4, -3)
+REACHED = (1, -1, 2, -2, 3, -3)
 MESH = pl.DeviceIdType.MESH
 F32 = jnp.float32
 BF16 = jnp.bfloat16
@@ -106,19 +112,16 @@
     out_ref, shift_ref,
     v_ref, fx, ix, fy, iy, fz, iz, flip_z, flip_y,
     send_f, recv_f, spec, moved, first_f, last_f, first_t, last_t, other, pair,
-    ring_r, ring_l, sent_r, sent_l, tmpl,
+    sums_in, sums_out, tmpl,
     send_i, recv_i, scores, stats_out, stats_in, ramp_zy, ramp_x,
     load_sem, fwd_send, fwd_recv, inv_send, inv_recv, st_send, st_recv,
-    oc_send, oc_recv, rr_send, rr_recv, rl_send, rl_recv,
-    gr_send, gr_recv, gl_send, gl_recv, go_send, go_recv,
+    oc_send, oc_recv, sum_send, sum_recv, mean_send, mean_recv, go_send, go_recv,
 ):
     s = lax.axis_index("space")
     t = lax.axis_index("tm")
     core = t % 2
     chip = t // 2
     mate = chip * 2 + 1 - core
-    right = ((chip + 1) % CHIPS) * 2 + core
-    left = ((chip + CHIPS - 1) % CHIPS) * 2 + core
 
     loads = [
         pltpu.make_async_copy(source, target, load_sem.at[i])
@@ -139,8 +142,10 @@
         return carry
 
     lax.fori_loop(1, SPACE, greet, 0)
-    for member in (mate, right, left):
+    for offset in REACHED:
+        member = ((chip + CHIPS + offset) % CHIPS) * 2 + core
         pl.semaphore_signal(barrier, inc=1, device_id={"tm": member}, device_id_type=MESH)
+    pl.semaphore_signal(barrier, inc=1, device_id={"tm": mate}, device_id_type=MESH)
 
     row = lax.broadcasted_iota(jnp.int32, (2 * Z, 128), 0)
     first_part = (row // SLABS) % 2 == 0
@@ -167,7 +172,7 @@
                     part * (X // 2) : (part + 1) * (X // 2), i * 128 : (i + 1) * 128
                 ]
 
-    pl.semaphore_wait(barrier, SPACE + 2)
+    pl.semaphore_wait(barrier, SPACE + len(REACHED))
 
     def exchange_part(source, target, send_sem, recv_sem, q):
         def one(i, carry):
@@ -277,17 +282,15 @@
         def swap():
             return to_tm(source.at[half_rows(q, 1 - core)], other.at[it, q], oc_send.at[it, q], oc_recv.at[it, q], mate)
 
-        def sum_r(outgoing, k):
-            return to_tm(outgoing, ring_r.at[it, q, k], rr_send.at[it, q, k], rr_recv.at[it, q, k], right)
-
-        def sum_l(outgoing, k):
-            return to_tm(outgoing, ring_l.at[it, q, k], rl_send.at[it, q, k], rl_recv.at[it, q, k], left)
-
-        def mean_r(i, k):
-            return to_tm(mean_unit(i), mean_unit(i), gr_send.at[it, q, k], gr_recv.at[it, q, k], right)
-
-        def mean_l(i, k):
-            return to_tm(mean_unit(i), mean_unit(i), gl_send.at[it, q, k], gl_recv.at[it, q, k], left)
+        def chip_at(offset):
+            return ((chip + CHIPS + offset) % CHIPS) * 2 + core
+
+        def sum_copy(outgoing, k, offset):
+            return to_tm(outgoing, sums_in.at[it, q, k], sum_send.at[it, q, k], sum_recv.at[it, q, k], chip_at(offset))
+
+        def mean_copy(i, k, offset):
+            ref = mean_unit(chip + CHIPS + i)
+            return to_tm(ref, ref, mean_send.at[it, q, k], mean_recv.at[it, q, k], chip_at(offset))
 
         def to_mate(c):
             ref = tmpl.at[it, half_rows(q, c)]
@@ -299,54 +302,38 @@
         def step_pair():
             swap().wait_recv()
             pair[it, q] = source[half_rows(q, core), :] + other[it, q]
-            start(sum_r(pair_unit(chip + 4), 0))
-            start(sum_l(pair_unit(chip + CHIPS - 3), 0))
-
-        def step_sum(k):
-            def run():
-                sum_r(sent_r.at[it, q, k - 1], k - 1).wait_recv()
-                sent_r[it, q, k - 1] = pair_unit(chip + 4 - k)[...] + ring_r[it, q, k - 1]
-                start(sum_r(sent_r.at[it, q, k - 1], k))
-                if k < 3:
-                    sum_l(sent_l.at[it, q, k - 1], k - 1).wait_recv()
-                    sent_l[it, q, k - 1] = pair_unit(chip + CHIPS - 3 + k)[...] + ring_l[it, q, k - 1]
-                    start(sum_l(sent_l.at[it, q, k - 1], k))
-
-            return run
+            for k, (i, offset) in enumerate(FIRST_SUMS):
+                start(sum_copy(pair_unit(chip + CHIPS + i), k, offset))
+
+        def step_merge():
+            for k, i in enumerate(MERGED):
+                sum_copy(sums_out.at[it, q, k], k, i).wait_recv()
+                sums_out[it, q, k] = pair_unit(chip + CHIPS + i)[...] + sums_in[it, q, k]
+                start(sum_copy(sums_out.at[it, q, k], 4 + k, i))
 
         def step_mean():
-            sum_l(ring_l.at[it, q, 2], 2).wait_recv()
-            sum_r(ring_r.at[it, q, 3], 3).wait_recv()
-            total = pair_unit(chip)[...] + (ring_r[it, q, 3] + ring_l[it, q, 2])
+            total = pair_unit(chip)[...]
+            for k in range(3, 7):
+                sum_copy(sums_in.at[it, q, k], k, 1).wait_recv()
+                total = total + sums_in[it, q, k]
             tmpl[it, rows_of((2 * q + core) * HALF + chip * UNIT, UNIT), :] = total * (1.0 / FRAMES)
-            start(mean_r(chip, 0))
-            start(mean_l(chip, 0))
-
-        def step_pass(k):
-            def run():
-                mean_r(chip + CHIPS - k, k - 1).wait_recv()
-                start(mean_r(chip + CHIPS - k, k))
-                if k < 3:
-                    mean_l(chip + k, k - 1).wait_recv()
-                    start(mean_l(chip + k, k))
-
-            return run
+            for k, offset in enumerate(MEANS):
+                start(mean_copy(0, k, offset))
+
+        def step_pass():
+            for k, (i, offset) in enumerate(PASSED):
+                mean_copy(i, k, 1).wait_recv()
+                start(mean_copy(i, 4 + k, offset))
 
         def step_share():
-            mean_l(chip + 3, 2).wait_recv()
-            mean_r(chip + 4, 3).wait_recv()
+            for k, i in enumerate(LAST_MEANS):
+                mean_copy(i, 3 + k, 1).wait_recv()
             start(to_mate(core))
 
         def step_end():
             to_mate(1 - core).wait_recv()
 
-        return (
-            [step_swap, step_pair]
-            + [step_sum(k) for k in (1, 2, 3)]
-            + [step_mean]
-            + [step_pass(k) for k in (1, 2, 3)]
-            + [step_share, step_end]
-        )
+        return [step_swap, step_pair, step_merge, step_mean, step_pass, step_share, step_end]
 
     def whiten(f_re, f_im, t_re, t_im):
         p_re = f_re * t_re + f_im * t_im
@@ -611,10 +598,8 @@
             pltpu.VMEM((ITERS, 2 * Z, 128), F32),
             pltpu.VMEM((ITERS, NQ, HALF, 128), F32),
             pltpu.VMEM((ITERS, NQ, HALF, 128), F32),
-            pltpu.VMEM((ITERS, NQ, 4, UNIT, 128), F32),
+            pltpu.VMEM((ITERS, NQ, 7, UNIT, 128), F32),
             pltpu.VMEM((ITERS, NQ, 3, UNIT, 128), F32),
-            pltpu.VMEM((ITERS, NQ, 3, UNIT, 128), F32),
-            pltpu.VMEM((ITERS, NQ, 2, UNIT, 128), F32),
             pltpu.VMEM((ITERS, slots, 128), F32),
             pltpu.VMEM((ITERS + 1, ROWS, 128), F32),
             pltpu.VMEM((ITERS + 1, ROWS, 128), F32),
@@ -628,10 +613,8 @@
             dma((ITERS + 1, NQ, SPACE)), dma((ITERS + 1, NQ, SPACE)),
             dma((ITERS, SPACE)), dma((ITERS, SPACE)),
             dma((ITERS, NQ)), dma((ITERS, NQ)),
-            dma((ITERS, NQ, 4)), dma((ITERS, NQ, 4)),
-            dma((ITERS, NQ, 3)), dma((ITERS, NQ, 3)),
-            dma((ITERS, NQ, 4)), dma((ITERS, NQ, 4)),
-            dma((ITERS, NQ, 3)), dma((ITERS, NQ, 3)),
+            dma((ITERS, NQ, 7)), dma((ITERS, NQ, 7)),
+            dma((ITERS, NQ, 7)), dma((ITERS, NQ, 7)),
             dma((ITERS, NQ)), dma((ITERS, NQ)),
         ],
         compiler_params=pltpu.CompilerParams(

time: 149 us -> 145 us (0.973)
  Pallas kernels: 146 us -> 141 us
    pallas_call x1, Pallas kernels: 146 us -> 141 us  [body(): pl.pallas_call(kernel, out_shape=(jax.ShapeDtypeStruct((SLABS, X, Y), F32...]
where the time goes in v3:
time: 145 us
  Pallas kernels  141 us (97%)
  local copies, waits for them, and re-layouts  2.78 us (2%)
    pallas_call x1, Pallas kernels, body(): pl.pallas_call(kernel, out_shape=(jax.ShapeDtypeStruct((SLABS, X, Y), F32...  141 us

profile of v3, /device:TPU:1, one launch (start us, length us, event | category | flops | bytes accessed | tf_op | source)
XLA Modules:
  0.0 144.8 jit_solution(16252521237610687749)
XLA Ops:
  0.6 141.4 %register.1 = (f32[4,512,128]{2,1,0:T(8,128)}, f32[1,3]{1,0:T(1,128)}) custom-call(f32[4,512,128]{2,1,0:T(8,128)} %bitcast.3, bf16[2,512,512]{2,1,0:T(8,128)(2,1)} %constant.16.clone.fx_hbm, bf16[2,512,512]{2,1,0:T(8,128)(2,1)} %constant.17.clone.ix_hbm, bf16[2,256,256]{2,1,0:T(8,128)(2,1)} %constant.18.clone.fy_hbm, ...), custom_call_target="tpu_custom_call" | custom-call | tf_op jit(solution)/shard_map/register/pallas_call | solution.py:580
  142.0 0.0 copy-start
  142.0 2.3 %copy.13 = f32[1,4,512,128]{3,2,1,0:T(8,128)} copy(f32[1,4,512,128]{3,2,1,0:T(8,128)} %bitcast.2) | data formatting | bytes 2097152
  144.3 0.0 copy-done
  144.3 0.5 copy.14
Async XLA Ops:
  142.0 2.3 %copy-start = (f32[1,3]{1,0:T(1,128)S(1)}, f32[1,3]{1,0:T(1,128)}, u32[]{:S(2)}) copy-start(f32[1,3]{1,0:T(1,128)} %get-tuple-element.9) | copy-start | bytes 40

commit v4 on v3

--- a/solution.py
+++ b/solution.py
@@ -28,13 +28,16 @@
 PART = MSG // NQ
 HALF = SLOTS // NQ * Z
 UNIT = HALF // CHIPS
-PAIRS = SLOTS // 2 // NQ
+GROUP = 4
+GROUPS = SLOTS // NQ // GROUP
 FIRST_SUMS = ((2, 1), (4, 1), (-3, -1), (-1, -1))
 MERGED = (1, 3, -2)
 MEANS = (-1, -3, 2, 1)
 PASSED = ((1, -1), (3, -1), (-2, 1))
 LAST_MEANS = (-1, 2, 4, -3)
 REACHED = (1, -1, 2, -2, 3, -3)
+SPACING = (3.0, 1.0)
+STEP = 3.5
 MESH = pl.DeviceIdType.MESH
 F32 = jnp.float32
 BF16 = jnp.bfloat16
@@ -226,32 +229,33 @@
     def part_rows(value):
         return jnp.concatenate([value[:, :128], value[:, 128:]], axis=0)
 
-    def spectrum_two(a, b):
-        zed = table_dot(fz, jnp.concatenate([a, b], axis=1))
-        lines = jnp.concatenate([complex_rows(zed[:, :128]), complex_rows(zed[:, 128:])], axis=0)
-        freq = dot_table(lines, fy)
-        return part_rows(freq[:Z]), part_rows(freq[Z:])
+    def spectrum_of(slots):
+        zed = table_dot(fz, jnp.concatenate(slots, axis=1))
+        lines = [complex_rows(zed[:, i * 128 : (i + 1) * 128]) for i in range(len(slots))]
+        freq = dot_table(jnp.concatenate(lines, axis=0), fy)
+        return [part_rows(freq[i * Z : (i + 1) * Z]) for i in range(len(slots))]
 
     def slot_rows(j):
         return rows_of(j * 2 * Z, 2 * Z)
 
-    def spectrum_pair(i, carry):
-        j = 2 * i
-        a, b = spectrum_two(load_slot(j), load_slot(j + 1))
-        spec[slot_rows(j), :] = a
-        spec[slot_rows(j + 1), :] = b
+    def spectrum_group(i, carry):
+        group = [GROUP * i + k for k in range(GROUP)]
+        for j, value in zip(group, spectrum_of([load_slot(j) for j in group])):
+            spec[slot_rows(j), :] = value
         return carry
 
     owner = jnp.where(s == 0, 1.0, 0.0)
 
     def forward_part(q):
         wait_part(send_f, recv_f, fwd_send, fwd_recv, q)
-        lax.fori_loop(q * PAIRS, (q + 1) * PAIRS, spectrum_pair, 0)
+        lax.fori_loop(q * GROUPS, (q + 1) * GROUPS, spectrum_group, 0)
         if q == 0:
             slot = load_slot(0)
             keep = jnp.where(first_part, 1.0, 1.0 - owner)
             rolled = jnp.concatenate([slot[SLABS:], slot[:SLABS]], axis=0)
-            first_f[...], last_f[...] = spectrum_two(slot * keep, rolled * jnp.where(first_part, owner, 0.0))
+            first_f[...], last_f[...] = spectrum_of(
+                [slot * keep, rolled * jnp.where(first_part, owner, 0.0)]
+            )
 
     sends = []
 
@@ -376,19 +380,19 @@
             last = back([last_values()])
             last = jnp.concatenate([last[2 * Z - SLABS :], last[: 2 * Z - SLABS]], axis=0)
 
-        def pair_back(i, carry):
-            j = 2 * i
-            planes = back([slot_values(j), slot_values(j + 1)])
-            values = [planes[:, :128], planes[:, 128:]]
-            if q == 0:
-                keep = jnp.where(first_part, 1.0, jnp.where(s + j == 0, 0.0, 1.0))
-                values[0] = values[0] * keep + last * (1.0 - keep)
-            for k in range(2):
+        def group_back(i, carry):
+            group = [GROUP * i + k for k in range(GROUP)]
+            planes = back([slot_values(j) for j in group])
+            for k, j in enumerate(group):
+                value = planes[:, k * 128 : (k + 1) * 128]
+                if q == 0 and k == 0:
+                    keep = jnp.where(first_part, 1.0, jnp.where(s + j == 0, 0.0, 1.0))
+                    value = value * keep + last * (1.0 - keep)
                 for d in range(SPACE):
-                    send_i[n, rows_of(d * MSG + (j + k) * 8, 8), :] = values[k][8 * d : 8 * d + 8]
-            return carry
-
-        lax.fori_loop(q * PAIRS, (q + 1) * PAIRS, pair_back, 0)
+                    send_i[n, rows_of(d * MSG + j * 8, 8), :] = value[8 * d : 8 * d + 8]
+            return carry
+
+        lax.fori_loop(q * GROUPS, (q + 1) * GROUPS, group_back, 0)
         exchange_part(send_i.at[n], recv_i.at[n], inv_send.at[n], inv_recv.at[n], q)
 
     def inverse_wait(n):
@@ -498,7 +502,7 @@
         return carry
 
     def shift_part(q):
-        lax.fori_loop(q * 2 * PAIRS, (q + 1) * 2 * PAIRS, shift_one, 0)
+        lax.fori_loop(q * GROUPS * GROUP, (q + 1) * GROUPS * GROUP, shift_one, 0)
         if q == 0:
             moved[slot_rows(0), :] = packed(halves(moved[slot_rows(0), :]), shifted_last())
 
@@ -524,11 +528,11 @@
             steps = sum_steps(it, q, moved if it > 0 else spec)
             return [lambda: (begin(), steps[0]())] + steps[1:-1] + [lambda: (steps[-1](), end())]
 
-        plan = [part_steps(q) for q in range(NQ)]
-        for wave in range(NQ + len(plan[0]) - 1):
-            for q in range(NQ):
-                if 0 <= wave - q < len(plan[q]):
-                    plan[q][wave - q]()
+        plan = [
+            (SPACING[it] * q + STEP * k, q, step) for q in range(NQ) for k, step in enumerate(part_steps(q))
+        ]
+        for _, _, step in sorted(plan, key=lambda entry: entry[:2]):
+            step()
         inverse_wait(it)
         shifts = centroid(it)
         make_ramp(shifts)

time: 145 us -> 135 us (0.931); the launches traced: 145 us -> 133 us
  Pallas kernels: 141 us -> 130 us
    pallas_call x1, Pallas kernels: 141 us -> 130 us  [body(): pl.pallas_call(kernel, out_shape=(jax.ShapeDtypeStruct((SLABS, X, Y), F32...]
where the time goes in v4:
time: 135 us; the launch traced here: 133 us
  Pallas kernels  130 us (96%)
  local copies, waits for them, and re-layouts  2.78 us (2%)
    pallas_call x1, Pallas kernels, body(): pl.pallas_call(kernel, out_shape=(jax.ShapeDtypeStruct((SLABS, X, Y), F32...  130 us
    unnamed x4, local copies, waits for them, and re-layouts  2.78 us

profile of v4, /device:TPU:1, one launch (start us, length us, event | category | flops | bytes accessed | tf_op | source)
XLA Modules:
  0.0 133.3 jit_solution(8162864137003904224)
XLA Ops:
  0.6 129.9 %register.1 = (f32[4,512,128]{2,1,0:T(8,128)}, f32[1,3]{1,0:T(1,128)}) custom-call(f32[4,512,128]{2,1,0:T(8,128)} %bitcast.3, bf16[2,512,512]{2,1,0:T(8,128)(2,1)} %constant.16.clone.fx_hbm, bf16[2,512,512]{2,1,0:T(8,128)(2,1)} %constant.17.clone.ix_hbm, bf16[2,256,256]{2,1,0:T(8,128)(2,1)} %constant.18.clone.fy_hbm, ...), custom_call_target="tpu_custom_call" | custom-call | tf_op jit(solution)/shard_map/register/pallas_call | solution.py:584
  130.5 0.0 copy-start
  130.5 2.3 %copy.13 = f32[1,4,512,128]{3,2,1,0:T(8,128)} copy(f32[1,4,512,128]{3,2,1,0:T(8,128)} %bitcast.2) | data formatting | bytes 2097152
  132.8 0.0 copy-done
  132.8 0.5 copy.14
Async XLA Ops:
  130.5 2.3 %copy-start = (f32[1,3]{1,0:T(1,128)S(1)}, f32[1,3]{1,0:T(1,128)}, u32[]{:S(2)}) copy-start(f32[1,3]{1,0:T(1,128)} %get-tuple-element.9) | copy-start | bytes 40

commit v5 on v4

--- a/solution.py
+++ b/solution.py
@@ -71,11 +71,27 @@
     forward_z = forward_z[:, order]
     inverse_z = inverse_z[order, :]
 
-    out = []
-    for table in (forward_x, inverse_x, forward_y, inverse_y, forward_z, inverse_z):
+    slots = np.arange(X // 2).reshape(SPACE, 2, NQ // 2, SLOTS // NQ).transpose(1, 2, 0, 3).reshape(2, 1, -1)
+    columns = slots + np.arange(2)[None, :, None] * (X // 2)
+
+    def two(table):
         high = table.astype(np.float32).astype(ml_dtypes.bfloat16)
-        low = (table - high.astype(np.float64)).astype(np.float32).astype(ml_dtypes.bfloat16)
-        out.append(np.stack([high, low]))
+        return high, (table - high.astype(np.float64)).astype(np.float32).astype(ml_dtypes.bfloat16)
+
+    def block(table):
+        high, low = two(table)
+        return np.concatenate(
+            [np.concatenate([high, high], axis=1), np.concatenate([low, np.zeros_like(low)], axis=1)]
+        )
+
+    out = [
+        np.concatenate(two(forward_x)),
+        np.stack([np.concatenate(two(inverse_x[:, half.reshape(-1)])) for half in columns]),
+        np.stack(two(forward_y)),
+        np.stack(two(inverse_y)),
+        block(forward_z),
+        block(inverse_z),
+    ]
     flips = [np.zeros((n, n), ml_dtypes.bfloat16) for n in (Z, Y)]
     for flip in flips:
         flip[np.arange(len(flip)), -np.arange(len(flip))] = 1.0
@@ -91,18 +107,28 @@
     return jnp.dot(a, b, preferred_element_type=F32)
 
 
-def table_dot(table, data):
+def x_dot(table, data):
+    n = table.shape[0] // 2
     data_high, data_low = split(data)
-    return dot(table[0], data_high) + (dot(table[0], data_low) + dot(table[1], data_high))
-
-
-def dot_table(data, table):
+    both = dot(table, data_high)
+    return both[:n] + (both[n:] + dot(table[:n], data_low))
+
+
+def z_dot(table, data):
+    n = table.shape[0] // 2
+    both = dot(table, jnp.concatenate(split(data), axis=0))
+    return both[:n] + both[n:]
+
+
+def dot_y(data, table):
+    n = data.shape[0]
     data_high, data_low = split(data)
-    return dot(data_high, table[0]) + (dot(data_low, table[0]) + dot(data_high, table[1]))
+    both = dot(jnp.concatenate([data_high, data_low], axis=0), table[0])
+    return both[:n] + (both[n:] + dot(data_high, table[1]))
 
 
 def rows_of(start, count):
-    return pl.ds(pl.multiple_of(start, 8), count)
+    return pl.ds(start if isinstance(start, int) else pl.multiple_of(start, 8), count)
 
 
 def signed(index, n):
@@ -168,7 +194,7 @@
 
     for z in range(0, SLABS, 2):
         data = jnp.concatenate([v_ref[z], v_ref[z + 1]], axis=1)
-        result = table_dot(fx, data)
+        result = x_dot(fx[...], data)
         for i in range(2):
             for part in range(2):
                 send_f[pl.ds(part * SLABS + z + i, X // 2, stride=8), :] = result[
@@ -177,43 +203,45 @@
 
     pl.semaphore_wait(barrier, SPACE + len(REACHED))
 
-    def exchange_part(source, target, send_sem, recv_sem, q):
+    def by_device(device, q):
+        return device * MSG + q * PART
+
+    def by_part(device, q):
+        return (q * SPACE + device) * PART
+
+    def exchange_part(source, target, send_sem, recv_sem, q, place):
         def one(i, carry):
             d = (s + i) % SPACE
             to_space(
-                source, d * MSG + q * PART, target, s * MSG + q * PART,
-                send_sem.at[q, d], recv_sem.at[q, s], d, PART,
+                source, by_device(d, q), target, place(s, q), send_sem.at[q, d], recv_sem.at[q, s], d, PART
             ).start()
             return carry
 
         lax.fori_loop(1, SPACE, one, 0)
-        mine = rows_of(s * MSG + q * PART, PART)
-        target[mine, :] = source[mine, :]
-
-    def wait_part(source, target, send_sem, recv_sem, q):
+        target[rows_of(place(s, q), PART), :] = source[rows_of(by_device(s, q), PART), :]
+
+    def wait_part(source, target, send_sem, recv_sem, q, place):
         def one(i, carry):
             d = (s + i) % SPACE
             to_space(
-                source, d * MSG + q * PART, target, d * MSG + q * PART,
-                send_sem.at[q, d], recv_sem.at[q, d], d, PART,
+                source, by_device(d, q), target, place(d, q), send_sem.at[q, d], recv_sem.at[q, d], d, PART
             ).wait_recv()
             return carry
 
         lax.fori_loop(1, SPACE, one, 0)
 
-    def wait_sent(source, target, send_sem, recv_sem, q):
+    def wait_sent(source, target, send_sem, recv_sem, q, place):
         def one(i, carry):
             d = (s + i) % SPACE
             to_space(
-                source, d * MSG + q * PART, target, s * MSG + q * PART,
-                send_sem.at[q, d], recv_sem.at[q, s], d, PART,
+                source, by_device(d, q), target, place(s, q), send_sem.at[q, d], recv_sem.at[q, s], d, PART
             ).wait_send()
             return carry
 
         lax.fori_loop(1, SPACE, one, 0)
 
     def send_all(q, carry):
-        exchange_part(send_f, recv_f, fwd_send, fwd_recv, q)
+        exchange_part(send_f, recv_f, fwd_send, fwd_recv, q, by_device)
         return carry
 
     lax.fori_loop(0, NQ, send_all, 0)
@@ -230,25 +258,24 @@
         return jnp.concatenate([value[:, :128], value[:, 128:]], axis=0)
 
     def spectrum_of(slots):
-        zed = table_dot(fz, jnp.concatenate(slots, axis=1))
+        zed = z_dot(fz[...], jnp.concatenate(slots, axis=1))
         lines = [complex_rows(zed[:, i * 128 : (i + 1) * 128]) for i in range(len(slots))]
-        freq = dot_table(jnp.concatenate(lines, axis=0), fy)
+        freq = dot_y(jnp.concatenate(lines, axis=0), fy)
         return [part_rows(freq[i * Z : (i + 1) * Z]) for i in range(len(slots))]
 
     def slot_rows(j):
         return rows_of(j * 2 * Z, 2 * Z)
 
-    def spectrum_group(i, carry):
-        group = [GROUP * i + k for k in range(GROUP)]
-        for j, value in zip(group, spectrum_of([load_slot(j) for j in group])):
-            spec[slot_rows(j), :] = value
-        return carry
+    def groups(q):
+        return [[GROUP * i + k for k in range(GROUP)] for i in range(q * GROUPS, (q + 1) * GROUPS)]
 
     owner = jnp.where(s == 0, 1.0, 0.0)
 
     def forward_part(q):
-        wait_part(send_f, recv_f, fwd_send, fwd_recv, q)
-        lax.fori_loop(q * GROUPS, (q + 1) * GROUPS, spectrum_group, 0)
+        wait_part(send_f, recv_f, fwd_send, fwd_recv, q, by_device)
+        for group in groups(q):
+            for j, value in zip(group, spectrum_of([load_slot(j) for j in group])):
+                spec[slot_rows(j), :] = value
         if q == 0:
             slot = load_slot(0)
             keep = jnp.where(first_part, 1.0, 1.0 - owner)
@@ -349,7 +376,7 @@
         return value[:Z], value[Z:]
 
     def slot_of(ref, first, j):
-        return halves(jnp.where(j == 0, first[...], ref[slot_rows(j), :]))
+        return halves(first[...] if j == 0 else ref[slot_rows(j), :])
 
     def packed(first, last):
         (f_re, f_im), (l_re, l_im) = first, last
@@ -371,56 +398,56 @@
 
     def back(values):
         lines = [jnp.concatenate([re, im], axis=1) for re, im in values]
-        lines = dot_table(jnp.concatenate(lines, axis=0), iy)
+        lines = dot_y(jnp.concatenate(lines, axis=0), iy)
         planes = [part_rows(lines[i * Z : (i + 1) * Z]) for i in range(len(values))]
-        return table_dot(iz, jnp.concatenate(planes, axis=1))
+        return z_dot(iz[...], jnp.concatenate(planes, axis=1))
 
     def inverse_part(n, q, slot_values, last_values):
         if q == 0:
             last = back([last_values()])
             last = jnp.concatenate([last[2 * Z - SLABS :], last[: 2 * Z - SLABS]], axis=0)
 
-        def group_back(i, carry):
-            group = [GROUP * i + k for k in range(GROUP)]
+        for group in groups(q):
             planes = back([slot_values(j) for j in group])
             for k, j in enumerate(group):
                 value = planes[:, k * 128 : (k + 1) * 128]
-                if q == 0 and k == 0:
-                    keep = jnp.where(first_part, 1.0, jnp.where(s + j == 0, 0.0, 1.0))
+                if j == 0:
+                    keep = jnp.where(first_part, 1.0, 1.0 - owner)
                     value = value * keep + last * (1.0 - keep)
                 for d in range(SPACE):
                     send_i[n, rows_of(d * MSG + j * 8, 8), :] = value[8 * d : 8 * d + 8]
+        exchange_part(send_i.at[n], recv_i.at[n], inv_send.at[n], inv_recv.at[n], q, by_part)
+
+    def inverse_x(n, target):
+        count = ROWS // 16
+
+        def wait_one(q, carry):
+            wait_part(send_i.at[n], recv_i.at[n], inv_send.at[n], inv_recv.at[n], q, by_part)
             return carry
 
-        lax.fori_loop(q * GROUPS, (q + 1) * GROUPS, group_back, 0)
-        exchange_part(send_i.at[n], recv_i.at[n], inv_send.at[n], inv_recv.at[n], q)
-
-    def inverse_wait(n):
-        def one(q, carry):
-            wait_part(send_i.at[n], recv_i.at[n], inv_send.at[n], inv_recv.at[n], q)
-            return carry
-
-        lax.fori_loop(0, NQ, one, 0)
-
-    def cells(n, z):
-        columns = []
-        for i in range(2):
-            parts = [
-                recv_i[n, pl.ds(part * SLABS + z + i, X // 2, stride=8), :] for part in range(2)
-            ]
-            columns.append(jnp.concatenate(parts, axis=0))
-        return table_dot(ix, jnp.concatenate(columns, axis=1))
+        for half in range(2):
+            lax.fori_loop(half * (NQ // 2), (half + 1) * (NQ // 2), wait_one, 0)
+            for z in range(0, SLABS, 2):
+                columns = []
+                for i in range(2):
+                    parts = [
+                        recv_i[n, pl.ds(half * count * 8 + part * SLABS + z + i, count, stride=8), :]
+                        for part in range(2)
+                    ]
+                    columns.append(jnp.concatenate(parts, axis=0))
+                value = x_dot(ix[half], jnp.concatenate(columns, axis=1))
+                for i in range(2):
+                    plane = value[:, i * 128 : (i + 1) * 128]
+                    target[z + i] = plane if half == 0 else target[z + i] + plane
 
     lane = lax.broadcasted_iota(jnp.int32, (1, 128), 1)
 
     def centroid(it):
         top = jnp.full((8, 128), -jnp.inf, F32)
-        for z in range(0, SLABS, 2):
-            value = cells(it, z) * SHARPNESS
-            for i in range(2):
-                plane = value[:, i * 128 : (i + 1) * 128]
-                scores[z + i] = plane
-                top = jnp.maximum(top, jnp.max(plane.reshape(X // 8, 8, 128), axis=0))
+        inverse_x(it, scores)
+        for z in range(SLABS):
+            top = jnp.maximum(top, jnp.max(scores[z].reshape(X // 8, 8, 128), axis=0))
+        top = top * SHARPNESS
         top = jnp.max(jnp.max(top, axis=0, keepdims=True), axis=1, keepdims=True)
         step = 128
         x_row = lax.broadcasted_iota(jnp.int32, (step, 128), 0)
@@ -429,7 +456,7 @@
         def weigh(i, carry):
             total, by_z, by_x = carry
             z, x = i // (X // step), (i % (X // step)) * step
-            weights = jnp.exp(scores[z, rows_of(x, step), :] - top)
+            weights = jnp.exp(scores[z, rows_of(x, step), :] * SHARPNESS - top)
             x_at = ((x + x_row + X // 2) % X - X // 2).astype(F32)
             z_at = ((s * SLABS + z + Z // 2) % Z - Z // 2).astype(F32)
             here = jnp.sum(weights.reshape(step // 8, 8, 128), axis=0)
@@ -497,12 +524,10 @@
         f_re, f_im = halves(last_f[...])
         return f_re * ramp_zy[0] - f_im * ramp_zy[1], f_re * ramp_zy[1] + f_im * ramp_zy[0]
 
-    def shift_one(j, carry):
-        moved[slot_rows(j), :] = jnp.concatenate(shifted_slot(j), axis=0)
-        return carry
-
     def shift_part(q):
-        lax.fori_loop(q * GROUPS * GROUP, (q + 1) * GROUPS * GROUP, shift_one, 0)
+        for group in groups(q):
+            for j in group:
+                moved[slot_rows(j), :] = jnp.concatenate(shifted_slot(j), axis=0)
         if q == 0:
             moved[slot_rows(0), :] = packed(halves(moved[slot_rows(0), :]), shifted_last())
 
@@ -533,17 +558,12 @@
         ]
         for _, _, step in sorted(plan, key=lambda entry: entry[:2]):
             step()
-        inverse_wait(it)
         shifts = centroid(it)
         make_ramp(shifts)
 
     for q in range(NQ):
         inverse_part(ITERS, q, shifted_slot, shifted_last)
-    inverse_wait(ITERS)
-    for z in range(0, SLABS, 2):
-        value = cells(ITERS, z)
-        for i in range(2):
-            out_ref[z + i] = value[:, i * 128 : (i + 1) * 128]
+    inverse_x(ITERS, out_ref)
     by_z, by_x, by_y = shifts
     line = jnp.where(lane == 0, by_z, jnp.where(lane == 1, by_x, by_y))
     shift_ref[...] = line[:, 0:3]
@@ -552,9 +572,9 @@
         copy.wait_send()
 
     def finish(q, carry):
-        wait_sent(send_f, recv_f, fwd_send, fwd_recv, q)
+        wait_sent(send_f, recv_f, fwd_send, fwd_recv, q, by_device)
         for n in range(ITERS + 1):
-            wait_sent(send_i.at[n], recv_i.at[n], inv_send.at[n], inv_recv.at[n], q)
+            wait_sent(send_i.at[n], recv_i.at[n], inv_send.at[n], inv_recv.at[n], q, by_part)
         return carry
 
     lax.fori_loop(0, NQ, finish, 0)

time: 135 us -> 133 us (0.985)
  Pallas kernels: 130 us -> 128 us
    pallas_call x1, Pallas kernels: 130 us -> 128 us  [body(): pl.pallas_call(kernel, out_shape=(jax.ShapeDtypeStruct((SLABS, X, Y), F32...]
where the time goes in v5:
time: 133 us; the launch traced here: 131 us
  Pallas kernels  128 us (96%)
  local copies, waits for them, and re-layouts  2.78 us (2%)
    pallas_call x1, Pallas kernels, body(): pl.pallas_call(kernel, out_shape=(jax.ShapeDtypeStruct((SLABS, X, Y), F32...  128 us
    unnamed x4, local copies, waits for them, and re-layouts  2.78 us

profile of v5, /device:TPU:1, one launch (start us, length us, event | category | flops | bytes accessed | tf_op | source)
XLA Modules:
  0.0 131.2 jit_solution(8063505737960192238)
XLA Ops:
  0.6 127.8 %register.1 = (f32[4,512,128]{2,1,0:T(8,128)}, f32[1,3]{1,0:T(1,128)}) custom-call(f32[4,512,128]{2,1,0:T(8,128)} %bitcast.3, bf16[1024,512]{1,0:T(8,128)(2,1)} %constant.16.clone.fx_hbm, bf16[2,1024,256]{2,1,0:T(8,128)(2,1)} %constant.17.clone.ix_hbm, bf16[2,256,256]{2,1,0:T(8,128)(2,1)} %constant.18.clone.fy_hbm, ...), custom_call_target="tpu_custom_call" | custom-call | tf_op jit(solution)/shard_map/register/pallas_call | solution.py:604
  128.4 0.0 copy-start
  128.4 2.3 %copy.13 = f32[1,4,512,128]{3,2,1,0:T(8,128)} copy(f32[1,4,512,128]{3,2,1,0:T(8,128)} %bitcast.2) | data formatting | bytes 2097152
  130.7 0.0 copy-done
  130.7 0.5 copy.14
Async XLA Ops:
  128.4 2.3 %copy-start = (f32[1,3]{1,0:T(1,128)S(1)}, f32[1,3]{1,0:T(1,128)}, u32[]{:S(2)}) copy-start(f32[1,3]{1,0:T(1,128)} %get-tuple-element.9) | copy-start | bytes 40

commit v6 on v5

--- a/solution.py
+++ b/solution.py
@@ -15,6 +15,7 @@
 Z = 64
 ITERS = 2
 FRAMES = 16
+NORM = 1.0 / (X * Y * Z)
 SHARPNESS = 256.0
 FLOOR = 0.05 * (X * Y * Z)
 
@@ -56,7 +57,7 @@
     forward_x = np.concatenate([cos_x, im])
     weight = np.full((X, 1), 2.0)
     weight[0] = weight[half] = 1.0
-    inverse_x = (forward_x * weight).T / (X * Y * Z)
+    inverse_x = (forward_x * weight).T
 
     a = angles(Y, np.arange(Y), np.arange(Y))
     c, s = np.cos(a), np.sin(a)
@@ -138,9 +139,9 @@
 
 def kernel(
     v_hbm, fx_hbm, ix_hbm, fy_hbm, iy_hbm, fz_hbm, iz_hbm, flip_z_hbm, flip_y_hbm,
-    out_ref, shift_ref,
+    out_hbm, shift_ref,
     v_ref, fx, ix, fy, iy, fz, iz, flip_z, flip_y,
-    send_f, recv_f, spec, moved, first_f, last_f, first_t, last_t, other, pair,
+    out_ref, out_sem, send_f, recv_f, spec, moved, first_f, last_f, first_t, last_t, other, pair,
     sums_in, sums_out, tmpl,
     send_i, recv_i, scores, stats_out, stats_in, ramp_zy, ramp_x,
     load_sem, fwd_send, fwd_recv, inv_send, inv_recv, st_send, st_recv,
@@ -304,6 +305,8 @@
         return rows_of((2 * q + c) * HALF, HALF)
 
     def sum_steps(it, q, source):
+        side = 1 - 2 * (q % 2)
+
         def pair_unit(i):
             return pair.at[it, q, rows_of((i % CHIPS) * UNIT, UNIT)]
 
@@ -314,13 +317,13 @@
             return to_tm(source.at[half_rows(q, 1 - core)], other.at[it, q], oc_send.at[it, q], oc_recv.at[it, q], mate)
 
         def chip_at(offset):
-            return ((chip + CHIPS + offset) % CHIPS) * 2 + core
+            return ((chip + CHIPS + side * offset) % CHIPS) * 2 + core
 
         def sum_copy(outgoing, k, offset):
             return to_tm(outgoing, sums_in.at[it, q, k], sum_send.at[it, q, k], sum_recv.at[it, q, k], chip_at(offset))
 
         def mean_copy(i, k, offset):
-            ref = mean_unit(chip + CHIPS + i)
+            ref = mean_unit(chip + CHIPS + side * i)
             return to_tm(ref, ref, mean_send.at[it, q, k], mean_recv.at[it, q, k], chip_at(offset))
 
         def to_mate(c):
@@ -334,17 +337,17 @@
             swap().wait_recv()
             pair[it, q] = source[half_rows(q, core), :] + other[it, q]
             for k, (i, offset) in enumerate(FIRST_SUMS):
-                start(sum_copy(pair_unit(chip + CHIPS + i), k, offset))
+                start(sum_copy(pair_unit(chip + CHIPS + side * i), k, offset))
 
         def step_merge():
             for k, i in enumerate(MERGED):
                 sum_copy(sums_out.at[it, q, k], k, i).wait_recv()
-                sums_out[it, q, k] = pair_unit(chip + CHIPS + i)[...] + sums_in[it, q, k]
-                start(sum_copy(sums_out.at[it, q, k], 4 + k, i))
+                sums_out[it, q, k] = pair_unit(chip + CHIPS + side * i)[...] + sums_in[it, q, k]
+                start(sum_copy(sums_out.at[it, q, k], len(FIRST_SUMS) + k, i))
 
         def step_mean():
             total = pair_unit(chip)[...]
-            for k in range(3, 7):
+            for k in range(len(MERGED), CHIPS - 1):
                 sum_copy(sums_in.at[it, q, k], k, 1).wait_recv()
                 total = total + sums_in[it, q, k]
             tmpl[it, rows_of((2 * q + core) * HALF + chip * UNIT, UNIT), :] = total * (1.0 / FRAMES)
@@ -354,17 +357,18 @@
         def step_pass():
             for k, (i, offset) in enumerate(PASSED):
                 mean_copy(i, k, 1).wait_recv()
-                start(mean_copy(i, 4 + k, offset))
+                start(mean_copy(i, len(MEANS) + k, offset))
 
         def step_share():
             for k, i in enumerate(LAST_MEANS):
-                mean_copy(i, 3 + k, 1).wait_recv()
+                mean_copy(i, len(PASSED) + k, 1).wait_recv()
             start(to_mate(core))
 
         def step_end():
             to_mate(1 - core).wait_recv()
 
-        return [step_swap, step_pair, step_merge, step_mean, step_pass, step_share, step_end]
+        steps = [step_swap, step_pair, step_merge, step_mean, step_pass, step_share, step_end]
+        return [step for step in steps if (MERGED or step is not step_merge) and (PASSED or step is not step_pass)]
 
     def whiten(f_re, f_im, t_re, t_im):
         p_re = f_re * t_re + f_im * t_im
@@ -417,6 +421,10 @@
                 for d in range(SPACE):
                     send_i[n, rows_of(d * MSG + j * 8, 8), :] = value[8 * d : 8 * d + 8]
         exchange_part(send_i.at[n], recv_i.at[n], inv_send.at[n], inv_recv.at[n], q, by_part)
+
+    def store_planes(z):
+        planes = pl.ds(z, 2)
+        return pltpu.make_async_copy(out_ref.at[planes], out_hbm.at[planes], out_sem.at[z // 2])
 
     def inverse_x(n, target):
         count = ROWS // 16
@@ -439,6 +447,8 @@
                 for i in range(2):
                     plane = value[:, i * 128 : (i + 1) * 128]
                     target[z + i] = plane if half == 0 else target[z + i] + plane
+                if half == 1 and n == ITERS:
+                    store_planes(z).start()
 
     lane = lax.broadcasted_iota(jnp.int32, (1, 128), 1)
 
@@ -447,7 +457,7 @@
         inverse_x(it, scores)
         for z in range(SLABS):
             top = jnp.maximum(top, jnp.max(scores[z].reshape(X // 8, 8, 128), axis=0))
-        top = top * SHARPNESS
+        top = top * (SHARPNESS * NORM)
         top = jnp.max(jnp.max(top, axis=0, keepdims=True), axis=1, keepdims=True)
         step = 128
         x_row = lax.broadcasted_iota(jnp.int32, (step, 128), 0)
@@ -456,7 +466,7 @@
         def weigh(i, carry):
             total, by_z, by_x = carry
             z, x = i // (X // step), (i % (X // step)) * step
-            weights = jnp.exp(scores[z, rows_of(x, step), :] * SHARPNESS - top)
+            weights = jnp.exp(scores[z, rows_of(x, step), :] * (SHARPNESS * NORM) - top)
             x_at = ((x + x_row + X // 2) % X - X // 2).astype(F32)
             z_at = ((s * SLABS + z + Z // 2) % Z - Z // 2).astype(F32)
             here = jnp.sum(weights.reshape(step // 8, 8, 128), axis=0)
@@ -570,6 +580,8 @@
 
     for copy in sends:
         copy.wait_send()
+    for z in range(0, SLABS, 2):
+        store_planes(z).wait()
 
     def finish(q, carry):
         wait_sent(send_f, recv_f, fwd_send, fwd_recv, q, by_device)
@@ -608,10 +620,12 @@
             jax.ShapeDtypeStruct((1, 3), F32),
         ),
         in_specs=[hbm] * (1 + len(consts)),
-        out_specs=(vmem, vmem),
+        out_specs=(hbm, vmem),
         scratch_shapes=[
             pltpu.VMEM((SLABS, X, Y), F32),
             *[pltpu.VMEM(table.shape, BF16) for table in consts],
+            pltpu.VMEM((SLABS, X, Y), F32),
+            dma((SLABS // 2,)),
             pltpu.VMEM((ROWS, 128), F32),
             pltpu.VMEM((ROWS, 128), F32),
             pltpu.VMEM((slots, 128), F32),
@@ -646,7 +660,7 @@
         ),
         name="register",
     )(volumes[0], *consts)
-    return corrected[None], shifts
+    return corrected[None] * NORM, shifts
 
 
 def solution(mesh):

time: 133 us -> 132 us (level)
  local copies, waits for them, and re-layouts: 2.78 us -> 0.51 us
  other arithmetic: 0 us -> 2.26 us
    mul x0 -> x1, other arithmetic: none -> 2.26 us  [body(): return (corrected[None] * NORM, shifts)]
    unnamed x4 -> x3, local copies, waits for them, and re-layouts: 2.78 us -> 0.51 us
where the time goes in v6:
time: 132 us; the launch traced here: 131 us
  Pallas kernels  128 us (97%)
  other arithmetic  2.26 us (2%)
    pallas_call x1, Pallas kernels, body(): pl.pallas_call(kernel, out_shape=(jax.ShapeDtypeStruct((SLABS, X, Y), F32...  128 us

profile of v6, /device:TPU:1, one launch (start us, length us, event | category | flops | bytes accessed | tf_op | source)
XLA Modules:
  0.0 130.9 jit_solution(2402900445259631858)
XLA Ops:
  0.6 127.5 %register.1 = (f32[4,512,128]{2,1,0:T(8,128)}, f32[1,3]{1,0:T(1,128)}) custom-call(f32[4,512,128]{2,1,0:T(8,128)} %bitcast.3, bf16[1024,512]{1,0:T(8,128)(2,1)} %constant.18.clone.fx_hbm, bf16[2,1024,256]{2,1,0:T(8,128)(2,1)} %constant.19.clone.ix_hbm, bf16[2,256,256]{2,1,0:T(8,128)(2,1)} %constant.20.clone.fy_hbm, ...), custom_call_target="tpu_custom_call" | custom-call | tf_op jit(solution)/shard_map/register/pallas_call | solution.py:616
  128.1 0.0 copy-start
  128.2 2.3 %multiply_bitcast_fusion = f32[1,4,512,128]{3,2,1,0:T(8,128)} fusion(f32[4,512,128]{2,1,0:T(8,128)} %get-tuple-element.4), kind=kLoop, calls=%fused_computation | loop fusion | flops 262144 | bytes 2097152 | tf_op jit(solution)/shard_map/mul | solution.py:663
  130.4 0.0 copy-done
  130.4 0.5 copy.12
Async XLA Ops:
  128.1 2.3 %copy-start = (f32[1,3]{1,0:T(1,128)S(1)}, f32[1,3]{1,0:T(1,128)}, u32[]{:S(2)}) copy-start(f32[1,3]{1,0:T(1,128)} %get-tuple-element.9) | copy-start | bytes 40

commit v7 on v6

--- a/solution.py
+++ b/solution.py
@@ -571,7 +571,7 @@
         shifts = centroid(it)
         make_ramp(shifts)
 
-    for q in range(NQ):
+    for q in (1, 0, *range(2, NQ)):
         inverse_part(ITERS, q, shifted_slot, shifted_last)
     inverse_x(ITERS, out_ref)
     by_z, by_x, by_y = shifts

time: 132 us -> 132 us (level)
  no operation moved by 1% of the time
where the time goes in v7:
time: 132 us; the launch traced here: 131 us
  Pallas kernels  127 us (96%)
  other arithmetic  2.26 us (2%)
    pallas_call x1, Pallas kernels, body(): pl.pallas_call(kernel, out_shape=(jax.ShapeDtypeStruct((SLABS, X, Y), F32...  127 us

profile of v7, /device:TPU:1, one launch (start us, length us, event | category | flops | bytes accessed | tf_op | source)
XLA Modules:
  0.0 130.8 jit_solution(2848496922247906057)
XLA Ops:
  0.6 127.3 %register.1 = (f32[4,512,128]{2,1,0:T(8,128)}, f32[1,3]{1,0:T(1,128)}) custom-call(f32[4,512,128]{2,1,0:T(8,128)} %bitcast.3, bf16[1024,512]{1,0:T(8,128)(2,1)} %constant.18.clone.fx_hbm, bf16[2,1024,256]{2,1,0:T(8,128)(2,1)} %constant.19.clone.ix_hbm, bf16[2,256,256]{2,1,0:T(8,128)(2,1)} %constant.20.clone.fy_hbm, ...), custom_call_target="tpu_custom_call" | custom-call | tf_op jit(solution)/shard_map/register/pallas_call | solution.py:616
  128.0 0.0 copy-start
  128.0 2.3 %multiply_bitcast_fusion = f32[1,4,512,128]{3,2,1,0:T(8,128)} fusion(f32[4,512,128]{2,1,0:T(8,128)} %get-tuple-element.4), kind=kLoop, calls=%fused_computation | loop fusion | flops 262144 | bytes 2097152 | tf_op jit(solution)/shard_map/mul | solution.py:663
  130.2 0.0 copy-done
  130.2 0.5 copy.12
Async XLA Ops:
  128.0 2.3 %copy-start = (f32[1,3]{1,0:T(1,128)S(1)}, f32[1,3]{1,0:T(1,128)}, u32[]{:S(2)}) copy-start(f32[1,3]{1,0:T(1,128)} %get-tuple-element.9) | copy-start | bytes 40
